TPU v7x, 32 devices: a whole 2x2x4 slice. The times are simulated.
32 devices in a mesh: ctx: 8 (over z, y), section: 2 (over core), tp: 2 (over x).
Axes of the slice: x: 2, y: 2, z: 4, core: 2. Of those that a mesh axis runs over, the one named last changes fastest.
Arguments:
- residual: bfloat16 [2048, 3584], P('ctx', 'tp'), may hold values from -6 to 6
- queries: bfloat16 [2, 2048, 2048], P('section', 'ctx', 'tp'), may hold values from -5 to 5
- keys: bfloat16 [2, 2048, 512], P('section', 'ctx', 'tp'), may hold values from -5 to 5
- window_values: bfloat16 [2048, 512], P('ctx', 'tp'), may hold values from -6 to 6
- mixing: bfloat16 [2, 2048, 3584], P('section', 'tp'), may hold values from -0.125 to 0.125
- norm_gain: bfloat16 [3584], replicated, may hold values from 0.5 to 1.5
- log_decay: float32 [2048, 16], P('ctx', 'tp'), may hold values from -1 to 0
- spike_counts: int32 [2048, 2048], P('ctx', 'tp'), may hold values from 0 to 3
- thresholds: float32 [2048], P('tp'), may hold values from 0.5 to 2
- lengths: int32 [8], replicated, may hold values from 128 to 256, as said below
Outputs:
- head_outputs: bfloat16 [2, 2048, 2048], P('section', 'ctx', 'tp')
- hidden: bfloat16 [2048, 3584], P('ctx', 'tp')
Inputs may be any that keep to these rules, and one draw needn't show every extreme that they name: `lengths`: the valid tokens of a shard come first; some shard is full in every draw.
All inputs are finite; a program needn't handle non-finite values.
Results may differ from a plain program's by a relative error of at most 0.015.
Values may be sent and summed in bfloat16 or wider, within the bound.
A program may use at most 128 MiB of HBM per device.

v0:
```python
import math

import jax
import jax.numpy as jnp
from jax import lax
from jax.sharding import PartitionSpec as P

HEAD = 128
WINDOW = 4096


def passed_along(x, axis, by):
    devices = lax.axis_size(axis)
    pairs = [(i, i + by) for i in range(devices) if 0 <= i + by < devices]
    return lax.ppermute(x, axis, pairs)


def entering(x, axis, join, neutral):
    place = lax.axis_index(axis)
    gathered = jax.tree.map(
        lambda a, kind: lax.all_gather(a.astype(kind), axis), x, (jnp.bfloat16, jnp.bfloat16)
    )
    state = jax.tree.map(lambda a, e: jnp.zeros_like(a) + jnp.asarray(e, a.dtype), x, neutral)

    def one(step, state):
        return join(
            state,
            jax.tree.map(
                lambda a, own: lax.dynamic_index_in_dim(a, step, 0, False).astype(own.dtype),
                gathered,
                x,
            ),
        )

    return lax.fori_loop(0, place, one, state)


def body(
    residual,
    queries,
    keys,
    window_values,
    mixing,
    norm_gain,
    log_decay,
    spike_counts,
    thresholds,
    lengths,
):
    section_index = lax.axis_index("section")
    shard_index = lax.axis_index("ctx")
    row_count = keys.shape[1]
    head_size = HEAD
    key_heads = keys.shape[2] // head_size
    query_head_rows = queries.shape[2] // head_size
    group_size = query_head_rows // key_heads
    span_blocks = WINDOW // row_count
    feature_count = mixing.shape[2]
    scale = 1.0 / math.sqrt(head_size)
    positions = jnp.arange(row_count, dtype=jnp.int32)
    valid_rows = positions < lengths[shard_index]
    own_keys = keys[0]
    earlier = [
        passed_along((own_keys, window_values), "ctx", distance + 1)
        for distance in range(span_blocks)
    ]
    key_blocks = jnp.stack([pair[0] for pair in earlier[::-1]] + [own_keys], 0)
    value_blocks = jnp.stack([pair[1] for pair in earlier[::-1]] + [window_values], 0)

    def window_layer(dummy_arg):
        query_rows = queries[0].reshape(row_count, key_heads, group_size, head_size)
        sources = shard_index - span_blocks + jnp.arange(span_blocks + 1, dtype=jnp.int32)
        block_valid = (sources[:, None] >= 0) & (
            positions[None, :] < lengths[jnp.clip(sources, 0, None)][:, None]
        )
        offsets = (span_blocks - jnp.arange(span_blocks + 1, dtype=jnp.int32)) * row_count
        base_distance = positions[:, None] - positions[None, :]

        def weight_step(carry, items):
            running, totals, best = carry
            scores = (
                jnp.einsum(
                    "rgjd,kgd->gjrk",
                    query_rows,
                    items[0].reshape(row_count, key_heads, head_size),
                    preferred_element_type=jnp.float32,
                )
                * scale
            )
            distance = base_distance + items[3]
            allowed = items[2][None, :] & (distance >= 0) & (distance < WINDOW)
            scores = jnp.where(allowed, scores, -1e30)
            new_best = jnp.maximum(best, jnp.max(scores, axis=-1))
            factor = jnp.exp(best - new_best)
            weights = jnp.where(allowed, jnp.exp(scores - new_best[..., None]), 0.0)
            blended = jnp.einsum(
                "gjrk,kgd->gjrd",
                weights.astype(jnp.bfloat16),
                items[1].reshape(row_count, key_heads, head_size),
                preferred_element_type=jnp.float32,
            )
            return (
                (
                    running * factor[..., None] + blended,
                    totals * factor + jnp.sum(weights, axis=-1),
                    new_best,
                ),
                None,
            )

        start_sums = (
            jnp.zeros((key_heads, group_size, row_count, head_size), jnp.float32),
            jnp.zeros((key_heads, group_size, row_count), jnp.float32),
            jnp.full((key_heads, group_size, row_count), -1e30, jnp.float32),
        )
        (blended, totals, unused_best), unused_sum = lax.scan(
            weight_step, start_sums, (key_blocks, value_blocks, block_valid, offsets)
        )
        attention = blended / jnp.maximum(totals, 1.0)[..., None]
        attention = attention.transpose(2, 0, 1, 3).reshape(row_count, query_head_rows * head_size)
        attention = jnp.where(valid_rows[:, None], attention, 0.0).astype(jnp.bfloat16)
        projected = jnp.dot(attention, mixing[0], preferred_element_type=jnp.float32)
        return (attention, projected)

    def window_skip(dummy_arg):
        return (
            jnp.zeros((row_count, query_head_rows * head_size), jnp.bfloat16),
            jnp.zeros((row_count, feature_count), jnp.float32),
        )

    attention, projected = lax.cond(section_index == 0, window_layer, window_skip, 0)
    share = lax.psum_scatter(
        projected.astype(jnp.bfloat16), "tp", scatter_dimension=1, tiled=True
    ).astype(jnp.float32)
    own_hidden = (share + residual.astype(jnp.float32)).astype(jnp.bfloat16)
    moved_share = passed_along(own_hidden, "section", 1)
    local_activations = jnp.where(section_index == 0, own_hidden, moved_share)
    complete_hidden_matrix = lax.all_gather(local_activations, "tp", axis=1, tiled=True)
    masked_keys = jnp.where(valid_rows[:, None], own_keys, jnp.zeros_like(own_keys)).reshape(
        row_count, key_heads, head_size
    )
    wide_keys = masked_keys.astype(jnp.float32)
    decays = log_decay * valid_rows[:, None].astype(jnp.float32)

    def linear_prepare(dummy_arg):
        wide = complete_hidden_matrix.astype(jnp.float32)
        normed = (
            wide
            * lax.rsqrt(jnp.mean(wide * wide, axis=-1, keepdims=True) + 1e-05)
            * norm_gain.astype(jnp.float32)
        ).astype(jnp.bfloat16)
        payload_vectors = lax.dot_general(
            normed, mixing[0], (((1,), (1,)), ((), ())), preferred_element_type=jnp.float32
        ).astype(jnp.bfloat16)
        cumulated = jnp.cumsum(decays, axis=0).reshape(row_count, key_heads, group_size)
        value_rows = payload_vectors.astype(jnp.float32).reshape(
            row_count, key_heads, group_size, head_size
        )
        fresh_state = jnp.einsum(
            "sgd,sgje->gdje",
            wide_keys,
            value_rows * jnp.exp(cumulated[-1] - cumulated)[..., None],
            precision=lax.Precision.HIGHEST,
        )
        return (payload_vectors, cumulated, fresh_state)

    def linear_skip(dummy_arg):
        return (
            jnp.zeros((row_count, query_head_rows * head_size), jnp.bfloat16),
            jnp.zeros((row_count, key_heads, group_size), jnp.float32),
            jnp.zeros((key_heads, head_size, group_size, head_size), jnp.float32),
        )

    payload_vectors, cumulated, fresh_state = lax.cond(
        section_index == 1, linear_prepare, linear_skip, 0
    )

    def chain(previous_entry, latter):
        return (
            previous_entry[0] + latter[0],
            previous_entry[1] * jnp.exp(latter[0])[:, None, :, None] + latter[1],
        )

    identity = (jnp.zeros((key_heads, group_size), jnp.float32), jnp.zeros_like(fresh_state))
    unused_total, incoming = entering((cumulated[-1], fresh_state), "ctx", chain, identity)

    def linear_finish(dummy_arg):
        query_narrow = queries[0].reshape(row_count, key_heads, group_size, head_size)
        query_rows = query_narrow.astype(jnp.float32)
        value_rows = payload_vectors.astype(jnp.float32).reshape(
            row_count, key_heads, group_size, head_size
        )
        inter = (
            jnp.einsum("rgjd,gdje->rgje", query_rows, incoming, precision=lax.Precision.HIGHEST)
            * jnp.exp(cumulated)[..., None]
        )
        products = jnp.einsum(
            "rgjd,sgd->gjrs", query_narrow, masked_keys, preferred_element_type=jnp.float32
        )
        ordered = cumulated.transpose(1, 2, 0)
        spread = ordered[..., :, None] - ordered[..., None, :]
        triangle = positions[:, None] >= positions[None, :]
        damping = jnp.where(triangle, jnp.exp(jnp.minimum(spread, 0.0)), 0.0)
        intra = jnp.einsum(
            "gjrs,sgje->rgje", products * damping, value_rows, precision=lax.Precision.HIGHEST
        )
        mixed = (inter + intra).reshape(row_count, query_head_rows, head_size)
        scaled = mixed * lax.rsqrt(jnp.mean(mixed * mixed, axis=-1, keepdims=True) + 1e-05)
        gating = spike_counts.astype(jnp.float32).reshape(
            row_count, query_head_rows, head_size
        ) * thresholds.reshape(query_head_rows, head_size)
        return jnp.where(
            valid_rows[:, None],
            (scaled * gating).reshape(row_count, query_head_rows * head_size),
            0.0,
        ).astype(jnp.bfloat16)

    def finish_skip(dummy_arg):
        return jnp.zeros((row_count, query_head_rows * head_size), jnp.bfloat16)

    gated = lax.cond(section_index == 1, linear_finish, finish_skip, 0)
    head_outputs = jnp.where(section_index == 0, attention, gated)[None]
    return (head_outputs, local_activations)


def solution(mesh):
    return jax.shard_map(
        body,
        mesh=mesh,
        in_specs=(
            P("ctx", "tp"),
            P("section", "ctx", "tp"),
            P("section", "ctx", "tp"),
            P("ctx", "tp"),
            P("section", "tp", None),
            P(),
            P("ctx", "tp"),
            P("ctx", "tp"),
            P("tp"),
            P(),
        ),
        out_specs=(P("section", "ctx", "tp"), P("ctx", "tp")),
        check_vma=False,
    )
```

profile of v0, /device:TPU:25, one launch (start us, length us, event | category | flops | bytes accessed | tf_op | source)
XLA Modules:
  0.0 347.5 jit_solution(17583788096226911408)
XLA Ops:
  19.2 1.5 collective-permute-done.10
  20.8 2.2 collective-permute-start.15
  23.7 9.3 %collective-permute-done.12 = bf16[256,256]{0,1:T(8,128)(2,1)S(1)} collective-permute-done((bf16[256,256]{0,1:T(8,128)(2,1)S(1)}, bf16[256,256]{0,1:T(8,128)(2,1)S(1)}, u32[]{:S(2)}, u32[]{:S(2)}) %collective-permute-start.12) | collective-permute-done | bytes 131104 | tf_op jit(solution)/shard_map/ppermute | solution.py:15
  38.4 1.4 collective-permute-start.5
  47.7 1.9 collective-permute-start.7
  51.6 2.3 collective-permute-done.5
  54.5 8.1 %collective-permute-done.6 = bf16[256,256]{0,1:T(8,128)(2,1)S(1)} collective-permute-done((bf16[256,256]{0,1:T(8,128)(2,1)S(1)}, bf16[256,256]{0,1:T(8,128)(2,1)S(1)}, u32[]{:S(2)}, u32[]{:S(2)}) %collective-permute-start.6) | collective-permute-done | bytes 131104 | tf_op jit(solution)/shard_map/ppermute | solution.py:15
  64.6 2.2 conditional.3
  64.6 1.4 broadcast.145
  66.9 156.9 %reduce-scatter.2.cloned.1.call-done = bf16[256,1792]{1,0:T(8,128)(2,1)} async-done(((bf16[256,3584]{1,0:T(8,128)(2,1)}), bf16[256,1792]{1,0:T(8,128)(2,1)}) %reduce-scatter.2.cloned.1.call-update) | async-done | bytes 917520 | tf_op jit(solution)/shard_map/reduce_scatter | solution.py:132
  223.8 1.4 add_convert_fusion
  225.2 1.3 collective-permute-start.16
  226.5 3.1 collective-permute-done.16
  232.0 28.5 %all-gather.4.cloned.1.call-done = bf16[256,3584]{1,0:T(8,128)(2,1)} async-done(((bf16[256,1792]{1,0:T(8,128)(2,1)}), bf16[256,3584]{1,0:T(8,128)(2,1)}) %all-gather.4.cloned.1.call-update) | async-done | bytes 1835024 | tf_op jit(solution)/shard_map/all_gather | solution.py:138
  260.5 13.4 %conditional.4 = (bf16[256,1024]{1,0:T(8,128)(2,1)}, f32[256,2,4]{0,2,1:T(4,128)}, bf16[2,128,4,128]{1,3,2,0:T(8,128)(2,1)S(1)}) conditional(s32[]{:T(128)} %convert_element_type.87, () %tuple.44, (bf16[256,3584]{1,0:T(8,128)(2,1)}, bf16[3584]{0:T(1024)(128)(2,1)S(1)}, bf16[1,1024,3584]{2,1,0:T(8,128)(2,1)}, f32[256,1]{0,1:T(1,128)S(1)}, ...), branch_computations={%region_7.8_spmd, %region_8.12_spmd} | conditional | flops 2288918272 | bytes 14811808 | solution.py:174
  263.0 1.9 fusion.25
  265.0 6.6 %fusion.31 = bf16[256,1024]{1,0:T(8,128)(2,1)} fusion(bf16[1,1024,3584]{2,1,0:T(8,128)(2,1)} %get-tuple-element.153, bf16[256,3584]{1,0:T(8,128)(2,1)} %get-tuple-element.151, f32[3584]{0:T(1024)S(1)} %convert_element_type.69, f32[256]{0:T(256)S(1)} %add_rsqrt_fusion.1), kind=kOutput, calls=%fused_computation.42 | convolution fusion | flops 1882980352 | bytes 9714688 | tf_op jit(solution)/shard_map/cond/branch_1_fun/dot_general | solution.py:152
  275.6 12.5 %all_gather.14 = bf16[8,2,4]{2,1,0:T(2,128)(2,1)S(1)} all-gather(bf16[1,2,4]{2,1,0:T(2,128)(2,1)S(1)} %copy.166), channel_id=1, replica_groups=mesh['ctx'=8,'section'=2,'tp'=2] {'ctx'}, dimensions={0}, use_global_device_ids=true | all-gather | bytes 144 | tf_op jit(solution)/shard_map/all_gather | solution.py:21
  288.2 33.9 %all-gather.6.cloned.1.call-done = bf16[16,128,4,128]{3,1,2,0:T(8,128)(2,1)} async-done(((bf16[2,128,4,128]{3,1,2,0:T(8,128)(2,1)}), bf16[16,128,4,128]{3,1,2,0:T(8,128)(2,1)}) %all-gather.6.cloned.1.call-update) | async-done | bytes 2097168 | tf_op jit(solution)/shard_map/all_gather | solution.py:21
  322.2 8.1 %while.27 = (s32[]{:T(128)}, f32[2,128,4,128]{3,2,1,0:T(4,128)S(1)}, s32[]{:T(128)}, bf16[8,2,4]{2,1,0:T(2,128)(2,1)S(1)}, bf16[8,2,128,4,128]{4,2,3,1,0:T(8,128)(2,1)}, /*index=5*/s32[]{:T(128)}, s32[]{:T(128)}, s32[]{:T(128)}) while((s32[]{:T(128)}, f32[2,128,4,128]{3,2,1,0:T(4,128)S(1)}, s32[]{:T(128)}, bf16[8,2,4]{2,1,0:T(2,128)(2,1)S(1)}, ...), condition=%wide.region_13.14_spmd, body=%wide.region_12.13_spmd.sunk | while | flops 393229 | bytes 1835215 | solution.py:35
  330.3 8.8 %conditional.5 = (bf16[256,1024]{1,0:T(8,128)(2,1)}) conditional(s32[]{:T(128)} %convert_element_type.87, () %tuple.43, (pred[256]{0:T(512)(128)(4,1)S(1)}, bf16[1,256,1024]{2,1,0:T(8,128)(2,1)S(1)}, f32[2,128,4,128]{3,2,1,0:T(4,128)S(1)}, f32[256,2,4]{0,2,1:T(4,128)}, bf16[256,2,128]{0,2,1:T(8,128)(2,1)S(1)}, /*index=5*/s32[256]{0:T(256)S(1)}, ...), branch_computations={%region_14.15_spmd, %region_15.17_spmd} | conditional | flops 1346963456 | bytes 21845284 | solution.py:221
  331.2 2.0 copy.142
  333.3 2.5 fusion.7
  339.1 1.9 select_bitcast_fusion
  (137 shorter events, 52.2 us)
Async XLA Ops:
  7.2 216.7 %reduce-scatter.2.cloned.1.call-start = ((), (), s32[]{:S(2)}) async-start(), calls=%async_computation.1 | async-start | bytes 2752512 | tf_op jit(solution)/shard_map/reduce_scatter | solution.py:132
  8.2 8.2 %collective-permute-start.8 = (bf16[256,256]{0,1:T(8,128)(2,1)S(1)}, bf16[256,256]{0,1:T(8,128)(2,1)S(1)}, u32[]{:S(2)}, u32[]{:S(2)}) collective-permute-start(bf16[256,256]{0,1:T(8,128)(2,1)S(1)} %copy.125), channel_id=1, source_target_pairs={} | collective-permute-start | bytes 393224 | tf_op jit(solution)/shard_map/ppermute | solution.py:15
  8.9 9.0 %collective-permute-start.9 = (bf16[256,256]{0,1:T(8,128)(2,1)S(1)}, bf16[256,256]{0,1:T(8,128)(2,1)S(1)}, u32[]{:S(2)}, u32[]{:S(2)}) collective-permute-start(bf16[256,256]{0,1:T(8,128)(2,1)S(1)} %copy.125), channel_id=1, source_target_pairs={{0,28},{1,29},{2,30},{3,31}} | collective-permute-start | bytes 393224 | tf_op jit(solution)/shard_map/ppermute | solution.py:15
  9.6 11.2 %collective-permute-start.10 = (bf16[256,256]{0,1:T(8,128)(2,1)S(1)}, bf16[256,256]{0,1:T(8,128)(2,1)S(1)}, u32[]{:S(2)}, u32[]{:S(2)}) collective-permute-start(bf16[256,256]{0,1:T(8,128)(2,1)S(1)} %copy.125), channel_id=1, source_target_pairs={{0,24},{4,28},{1,25},{5,29},{2,26},{6,30},{3,27},{7,31}} | collective-permute-start | bytes 393224 | tf_op jit(solution)/shard_map/ppermute | solution.py:15
  10.9 12.2 %collective-permute-start.11 = (bf16[256,256]{0,1:T(8,128)(2,1)S(1)}, bf16[256,256]{0,1:T(8,128)(2,1)S(1)}, u32[]{:S(2)}, u32[]{:S(2)}) collective-permute-start(bf16[256,256]{0,1:T(8,128)(2,1)S(1)} %copy.125), channel_id=1, source_target_pairs={{0,20},{4,24},{8,28},{1,21},{5,25},{9,29},{2,22},{6,26},{10,30},{3... | collective-permute-start | bytes 393224 | tf_op jit(solution)/shard_map/ppermute | solution.py:15
  12.2 20.9 %collective-permute-start.12 = (bf16[256,256]{0,1:T(8,128)(2,1)S(1)}, bf16[256,256]{0,1:T(8,128)(2,1)S(1)}, u32[]{:S(2)}, u32[]{:S(2)}) collective-permute-start(bf16[256,256]{0,1:T(8,128)(2,1)S(1)} %copy.125), channel_id=1, source_target_pairs={{0,16},{4,20},{8,24},{12,28},{1,17},{5,21},{9,25},{13,29},{2,18},{... | collective-permute-start | bytes 393224 | tf_op jit(solution)/shard_map/ppermute | solution.py:15
  16.4 17.9 %collective-permute-start.13 = (bf16[256,256]{0,1:T(8,128)(2,1)S(1)}, bf16[256,256]{0,1:T(8,128)(2,1)S(1)}, u32[]{:S(2)}, u32[]{:S(2)}) collective-permute-start(bf16[256,256]{0,1:T(8,128)(2,1)S(1)} %copy.125), channel_id=1, source_target_pairs={{0,12},{4,16},{8,20},{12,24},{16,28},{1,13},{5,17},{9,21},{13,25},... | collective-permute-start | bytes 393224 | tf_op jit(solution)/shard_map/ppermute | solution.py:15
  17.9 17.8 %collective-permute-start.14 = (bf16[256,256]{0,1:T(8,128)(2,1)S(1)}, bf16[256,256]{0,1:T(8,128)(2,1)S(1)}, u32[]{:S(2)}, u32[]{:S(2)}) collective-permute-start(bf16[256,256]{0,1:T(8,128)(2,1)S(1)} %copy.125), channel_id=1, source_target_pairs={{0,8},{4,12},{8,16},{12,20},{16,24},{20,28},{1,9},{5,13},{9,17},{1... | collective-permute-start | bytes 393224 | tf_op jit(solution)/shard_map/ppermute | solution.py:15
  20.8 16.2 %collective-permute-start.15 = (bf16[256,256]{0,1:T(8,128)(2,1)S(1)}, bf16[256,256]{0,1:T(8,128)(2,1)S(1)}, u32[]{:S(2)}, u32[]{:S(2)}) collective-permute-start(bf16[256,256]{0,1:T(8,128)(2,1)S(1)} %copy.125), channel_id=1, source_target_pairs={{0,4},{4,8},{8,12},{12,16},{16,20},{20,24},{24,28},{1,5},{5,9},{9,... | collective-permute-start | bytes 393224 | tf_op jit(solution)/shard_map/ppermute | solution.py:15
  23.0 15.3 %collective-permute-start = (bf16[256,256]{0,1:T(8,128)(2,1)S(1)}, bf16[256,256]{0,1:T(8,128)(2,1)S(1)}, u32[]{:S(2)}, u32[]{:S(2)}) collective-permute-start(bf16[256,256]{0,1:T(8,128)(2,1)S(1)} %bitcast.189), channel_id=1, source_target_pairs={} | collective-permute-start | bytes 393224 | tf_op jit(solution)/shard_map/ppermute | solution.py:15
  33.0 12.7 %collective-permute-start.1 = (bf16[256,256]{0,1:T(8,128)(2,1)S(1)}, bf16[256,256]{0,1:T(8,128)(2,1)S(1)}, u32[]{:S(2)}, u32[]{:S(2)}) collective-permute-start(bf16[256,256]{0,1:T(8,128)(2,1)S(1)} %bitcast.190), channel_id=1, source_target_pairs={{0,28},{1,29},{2,30},{3,31}} | collective-permute-start | bytes 393224 | tf_op jit(solution)/shard_map/ppermute | solution.py:15
  34.3 13.3 %collective-permute-start.2 = (bf16[256,256]{0,1:T(8,128)(2,1)S(1)}, bf16[256,256]{0,1:T(8,128)(2,1)S(1)}, u32[]{:S(2)}, u32[]{:S(2)}) collective-permute-start(bf16[256,256]{0,1:T(8,128)(2,1)S(1)} %bitcast.191), channel_id=1, source_target_pairs={{0,24},{4,28},{1,25},{5,29},{2,26},{6,30},{3,27},{7,31}} | collective-permute-start | bytes 393224 | tf_op jit(solution)/shard_map/ppermute | solution.py:15
  35.7 14.6 %collective-permute-start.3 = (bf16[256,256]{0,1:T(8,128)(2,1)S(1)}, bf16[256,256]{0,1:T(8,128)(2,1)S(1)}, u32[]{:S(2)}, u32[]{:S(2)}) collective-permute-start(bf16[256,256]{0,1:T(8,128)(2,1)S(1)} %bitcast.192), channel_id=1, source_target_pairs={{0,20},{4,24},{8,28},{1,21},{5,25},{9,29},{2,22},{6,26},{10,30},{3... | collective-permute-start | bytes 393224 | tf_op jit(solution)/shard_map/ppermute | solution.py:15
  37.0 13.9 %collective-permute-start.4 = (bf16[256,256]{0,1:T(8,128)(2,1)S(1)}, bf16[256,256]{0,1:T(8,128)(2,1)S(1)}, u32[]{:S(2)}, u32[]{:S(2)}) collective-permute-start(bf16[256,256]{0,1:T(8,128)(2,1)S(1)} %bitcast.193), channel_id=1, source_target_pairs={{0,16},{4,20},{8,24},{12,28},{1,17},{5,21},{9,25},{13,29},{2,18},{... | collective-permute-start | bytes 393224 | tf_op jit(solution)/shard_map/ppermute | solution.py:15
  38.3 26.3 %copy-start = (s32[8]{0:T(128)S(1)}, s32[8]{0:T(128)}, u32[]{:S(2)}) copy-start(s32[8]{0:T(128)} %param.29) | copy-start | bytes 100
  38.4 15.5 %collective-permute-start.5 = (bf16[256,256]{0,1:T(8,128)(2,1)S(1)}, bf16[256,256]{0,1:T(8,128)(2,1)S(1)}, u32[]{:S(2)}, u32[]{:S(2)}) collective-permute-start(bf16[256,256]{0,1:T(8,128)(2,1)S(1)} %bitcast.194), channel_id=1, source_target_pairs={{0,12},{4,16},{8,20},{12,24},{16,28},{1,13},{5,17},{9,21},{13,25},... | collective-permute-start | bytes 393224 | tf_op jit(solution)/shard_map/ppermute | solution.py:15
  45.7 16.9 %collective-permute-start.6 = (bf16[256,256]{0,1:T(8,128)(2,1)S(1)}, bf16[256,256]{0,1:T(8,128)(2,1)S(1)}, u32[]{:S(2)}, u32[]{:S(2)}) collective-permute-start(bf16[256,256]{0,1:T(8,128)(2,1)S(1)} %bitcast.195), channel_id=1, source_target_pairs={{0,8},{4,12},{8,16},{12,20},{16,24},{20,28},{1,9},{5,13},{9,17},{1... | collective-permute-start | bytes 393224 | tf_op jit(solution)/shard_map/ppermute | solution.py:15
  47.7 15.6 %collective-permute-start.7 = (bf16[256,256]{0,1:T(8,128)(2,1)S(1)}, bf16[256,256]{0,1:T(8,128)(2,1)S(1)}, u32[]{:S(2)}, u32[]{:S(2)}) collective-permute-start(bf16[256,256]{0,1:T(8,128)(2,1)S(1)} %bitcast.196), channel_id=1, source_target_pairs={{0,4},{4,8},{8,12},{12,16},{16,20},{20,24},{24,28},{1,5},{5,9},{9,... | collective-permute-start | bytes 393224 | tf_op jit(solution)/shard_map/ppermute | solution.py:15
  66.8 157.0 %copy-start.3 = (bf16[256,1792]{1,0:T(8,128)(2,1)S(1)}, bf16[256,1792]{1,0:T(8,128)(2,1)}, u32[]{:S(2)}) copy-start(bf16[256,1792]{1,0:T(8,128)(2,1)} %param.20) | copy-start | bytes 2752516
  66.9 193.6 %all-gather.4.cloned.1.call-start = ((), (), s32[]{:S(2)}) async-start(), calls=%async_computation.2 | async-start | bytes 2752512 | tf_op jit(solution)/shard_map/all_gather | solution.py:138
  225.2 35.3 %copy-start.6 = (bf16[3584]{0:T(1024)(128)(2,1)S(1)}, bf16[3584]{0:T(1024)(128)(2,1)}, u32[]{:S(2)}) copy-start(bf16[3584]{0:T(1024)(128)(2,1)} %param.25) | copy-start | bytes 21508
  225.2 35.3 %copy-start.7 = (f32[256,8]{0,1:T(8,128)S(1)}, f32[256,8]{0,1:T(8,128)}, u32[]{:S(2)}) copy-start(f32[256,8]{0,1:T(8,128)} %param.26) | copy-start | bytes 24580
  225.2 4.4 %collective-permute-start.16 = (bf16[256,1792]{1,0:T(8,128)(2,1)S(1)}, bf16[256,1792]{1,0:T(8,128)(2,1)S(1)}, u32[]{:S(2)}, u32[]{:S(2)}) collective-permute-start(bf16[256,1792]{1,0:T(8,128)(2,1)S(1)} %add_convert_fusion), channel_id=1, source_target_pairs={{0,2},{1,3},{4,6},{5,7},{8,10},{9,11},{12,14},{13,15},{16,18},{17,... | collective-permute-start | bytes 2752520 | tf_op jit(solution)/shard_map/ppermute | solution.py:15
  230.7 91.5 %all-gather.6.cloned.1.call-start = ((), (), s32[]{:S(2)}) async-start(), calls=%async_computation.3 | async-start | bytes 2359296 | tf_op jit(solution)/shard_map/all_gather | solution.py:21
  (4 other events, 44.1 us)
Sparse Core Ops, SparseCore 0:
  67.0 156.7 reduce-scatter.1
  230.8 29.6 all-gather.3
  274.9 47.1 all-gather.5
where the time goes:
time: 350 us; the launch traced here: 348 us
  waiting for transfers between devices  244 us (70%)
  local copies, waits for them, and re-layouts  31.5 us (9%)
  starting transfers between devices  21.2 us (6%)
  between operations  14.2 us (4%)
  blocking collectives  12.5 us (4%)
  other arithmetic  12 us (3%)
  matrix products  11.4 us (3%)
    reduce_scatter x1, waiting for transfers between devices, body(): lax.psum_scatter(projected.astype(jnp.bfloat16), 'tp', scatter_dimension=...  157 us
    all_gather x1, waiting for transfers between devices, entering(): lax.all_gather(a.astype(kind), axis)  33.9 us
    all_gather x1, waiting for transfers between devices, body(): lax.all_gather(local_activations, 'tp', axis=1, tiled=True)  28.5 us
    ppermute x17, waiting for transfers between devices, passed_along(): return lax.ppermute(x, axis, pairs)  25 us
    ppermute x17, starting transfers between devices, passed_along(): return lax.ppermute(x, axis, pairs)  21.1 us
    unnamed x49, local copies, waits for them, and re-layouts  12.9 us
    all_gather x1, blocking collectives, entering(): lax.all_gather(a.astype(kind), axis)  12.5 us
  transfers between devices with their start and end apart: 20, of which 9 were waited for; matrix products, arithmetic and copies ran while one was open for 4% of the time, Pallas kernels for 0%

commit v1 on v0

--- a/solution.py
+++ b/solution.py
@@ -1,8 +1,11 @@
+import functools
 import math
 
 import jax
 import jax.numpy as jnp
 from jax import lax
+from jax.experimental import pallas as pl
+from jax.experimental.pallas import tpu as pltpu
 from jax.sharding import PartitionSpec as P
 
 HEAD = 128
@@ -223,9 +226,611 @@
     return (head_outputs, local_activations)
 
 
+MESH = pl.DeviceIdType.MESH
+F32 = jnp.float32
+BF16 = jnp.bfloat16
+CHUNK = 256
+PAD = 16
+
+
+def nt(a, b):
+    return lax.dot_general(a, b, (((1,), (1,)), ((), ())), preferred_element_type=F32)
+
+
+def nn(a, b):
+    return jnp.dot(a, b, preferred_element_type=F32)
+
+
+def turned(x):
+    return jnp.transpose(x.astype(F32)).astype(BF16)
+
+
+def kernel(
+    n,
+    residual,
+    queries,
+    keys,
+    window_values,
+    mixing,
+    gain,
+    decay,
+    decay_t,
+    spikes,
+    thresholds,
+    lengths,
+    head_out,
+    hidden_out,
+    weights,
+    spike_buf,
+    kv,
+    moved_queries,
+    stacked,
+    top,
+    total,
+    blend,
+    attention,
+    terms,
+    own_terms,
+    far_terms,
+    residuals,
+    hidden_buf,
+    values_sum,
+    square_sum,
+    damped,
+    faded,
+    rest,
+    keys_t,
+    values,
+    states,
+    incoming,
+    passed,
+    mixed,
+    weights_sem,
+    spike_sem,
+    res_sem,
+    first_sem,
+    first_recv,
+    kv_send,
+    kv_recv,
+    kv_forward,
+    att_sem,
+    term_own_send,
+    term_far_send,
+    term_own_recv,
+    term_far_recv,
+    hid_send,
+    hid_recv,
+    state_send,
+    state_recv,
+    state_forward,
+):
+    c = lax.axis_index("ctx")
+    s = lax.axis_index("section")
+    p = lax.axis_index("tp")
+    odd = c % 2
+    step_to = 1 - 2 * odd
+    partner = c + step_to
+    rows = keys.shape[0]
+    half = residual.shape[1]
+    chunks_half = half // CHUNK
+    chunks = 2 * chunks_half
+    group = 4
+    wide = group * HEAD
+    factor = math.log2(math.e) / math.sqrt(HEAD)
+
+    barrier = pltpu.get_barrier_semaphore()
+    pl.semaphore_signal(barrier, inc=1, device_id={"section": 1 - s}, device_id_type=MESH)
+    pl.semaphore_signal(barrier, inc=1, device_id={"tp": 1 - p}, device_id_type=MESH)
+    pl.semaphore_signal(
+        barrier, inc=1, device_id={"section": 1 - s, "tp": 1 - p}, device_id_type=MESH
+    )
+    pl.semaphore_signal(barrier, inc=1, device_id={"ctx": partner}, device_id_type=MESH)
+    for k in range(1, n // 2):
+        pl.semaphore_signal(
+            barrier, inc=1, device_id={"ctx": (c + 2 * k) % n}, device_id_type=MESH
+        )
+
+    weights_copy = pltpu.make_async_copy(mixing, weights, weights_sem)
+    weights_copy.start()
+
+    own_len = lengths[c]
+
+    @pl.when(s == 0)
+    def _():
+        kv[0, 0:rows] = keys[:, 0:HEAD]
+        value_t = turned(window_values[:, 0:HEAD])
+        kv[0, rows : rows + HEAD] = value_t[:, 0:HEAD]
+        kv[0, rows + HEAD : rows + 2 * HEAD] = value_t[:, HEAD : 2 * HEAD]
+        for h in range(group):
+            stacked[h * rows : (h + 1) * rows, :] = queries[:, h * HEAD : (h + 1) * HEAD]
+
+    @pl.when(s == 1)
+    def _():
+        value_t = turned(window_values[:, HEAD : 2 * HEAD])
+        kv[0, rows : rows + HEAD] = value_t[:, 0:HEAD]
+        kv[0, rows + HEAD : rows + 2 * HEAD] = value_t[:, HEAD : 2 * HEAD]
+
+    pl.semaphore_wait(barrier, 3 + n // 2)
+
+    key_copy = pltpu.make_async_remote_copy(
+        src_ref=keys.at[:, HEAD : 2 * HEAD],
+        dst_ref=kv.at[0, 0:rows],
+        send_sem=first_sem.at[0],
+        recv_sem=first_recv.at[0],
+        device_id={"section": 1 - s},
+        device_id_type=MESH,
+    )
+    query_copy = pltpu.make_async_remote_copy(
+        src_ref=queries.at[:, wide : 2 * wide],
+        dst_ref=moved_queries,
+        send_sem=first_sem.at[1],
+        recv_sem=first_recv.at[1],
+        device_id={"section": 1 - s},
+        device_id_type=MESH,
+    )
+    residual_send = pltpu.make_async_remote_copy(
+        src_ref=residual,
+        dst_ref=residuals.at[p],
+        send_sem=res_sem.at[0],
+        recv_sem=res_sem.at[1],
+        device_id={"tp": 1 - p},
+        device_id_type=MESH,
+    )
+    residual_recv = pltpu.make_async_remote_copy(
+        src_ref=residual,
+        dst_ref=residuals.at[1 - p],
+        send_sem=res_sem.at[0],
+        recv_sem=res_sem.at[1],
+        device_id={"tp": 1 - p},
+        device_id_type=MESH,
+    )
+    residual_copy = pltpu.make_async_copy(residual, residuals.at[p], res_sem.at[2])
+    spike_copy = pltpu.make_async_copy(spikes, spike_buf, spike_sem)
+
+    @pl.when(s == 0)
+    def _():
+        key_copy.start()
+        query_copy.start()
+
+    @pl.when(s == 1)
+    def _():
+        residual_send.start()
+        residual_copy.start()
+        spike_copy.start()
+        key_copy.wait_recv()
+
+    def direct(buf, send, recv, k):
+        return pltpu.make_async_remote_copy(
+            src_ref=buf.at[0],
+            dst_ref=buf.at[2 * k],
+            send_sem=send.at[k],
+            recv_sem=recv.at[2 * k],
+            device_id={"ctx": lax.rem(c + 2 * k, n)},
+            device_id_type=MESH,
+        )
+
+    def forward(buf, send, recv, k):
+        return pltpu.make_async_remote_copy(
+            src_ref=buf.at[2 * k],
+            dst_ref=buf.at[2 * k + step_to],
+            send_sem=send.at[k],
+            recv_sem=recv.at[2 * k + step_to],
+            device_id={"ctx": partner},
+            device_id_type=MESH,
+        )
+
+    def arrival(buf, send, recv, slot):
+        return pltpu.make_async_remote_copy(
+            src_ref=buf.at[slot],
+            dst_ref=buf.at[slot],
+            send_sem=send.at[0],
+            recv_sem=recv.at[slot],
+            device_id={"ctx": partner},
+            device_id_type=MESH,
+        )
+
+    later = (n - 1 - c) // 2
+    before = c // 2
+
+    def send_own(buf, send, forward_sem, recv):
+        @pl.when(odd == 0)
+        def _():
+            forward(buf, forward_sem, recv, 0).start()
+
+        def one(k, carry):
+            direct(buf, send, recv, k).start()
+            return carry
+
+        lax.fori_loop(1, later + 1, one, 0)
+
+    def sent_own(buf, send, forward_sem, recv):
+        @pl.when(odd == 0)
+        def _():
+            forward(buf, forward_sem, recv, 0).wait_send()
+
+        def one(k, carry):
+            direct(buf, send, recv, k).wait_send()
+            return carry
+
+        lax.fori_loop(1, later + 1, one, 0)
+
+        def two(k, carry):
+            forward(buf, forward_sem, recv, k).wait_send()
+            return carry
+
+        lax.fori_loop(1, before + 1, two, 0)
+
+    send_own(kv, kv_send, kv_forward, kv_recv)
+
+    @pl.when(s == 1)
+    def _():
+        query_copy.wait_recv()
+        for h in range(group):
+            stacked[h * rows : (h + 1) * rows, :] = moved_queries[:, h * HEAD : (h + 1) * HEAD]
+
+    def attend(slot, first):
+        key_rows = kv[slot, 0:rows]
+        value_t = jnp.concatenate(
+            [kv[slot, rows : rows + HEAD], kv[slot, rows + HEAD : rows + 2 * HEAD]], axis=1
+        )
+        key_index = lax.broadcasted_iota(jnp.int32, (rows, rows), 0)
+        allowed = key_index < lengths[c - slot]
+        if first:
+            allowed = allowed & (key_index <= lax.broadcasted_iota(jnp.int32, (rows, rows), 1))
+        for h in range(group):
+            at = slice(h * rows, (h + 1) * rows)
+            scores = jnp.where(allowed, nt(key_rows, stacked[at, :]), -1e30)
+            best = jnp.max(scores, axis=0, keepdims=True)
+            if not first:
+                best = jnp.maximum(best, top[:, at])
+            part = jnp.exp2((scores - best) * factor)
+            part_sum = jnp.sum(part, axis=0, keepdims=True)
+            blended = nn(value_t, part.astype(BF16))
+            if first:
+                total[:, at] = part_sum
+                blend[:, at] = blended
+            else:
+                shrink = jnp.exp2((top[:, at] - best) * factor)
+                total[:, at] = total[:, at] * shrink + part_sum
+                blend[:, at] = blend[:, at] * shrink + blended
+            top[:, at] = best
+
+    attend(0, True)
+
+    def attend_pair(k, carry):
+        arrival(kv, kv_send, kv_recv, 2 * k).wait_recv()
+        forward(kv, kv_forward, kv_recv, k).start()
+        attend(2 * k, False)
+        arrival(kv, kv_send, kv_recv, 2 * k - 1).wait_recv()
+        attend(2 * k - 1, False)
+        return carry
+
+    lax.fori_loop(1, before + 1, attend_pair, 0)
+
+    @pl.when(odd == 1)
+    def _():
+        arrival(kv, kv_send, kv_recv, c).wait_recv()
+        attend(c, False)
+
+    row_lane = lax.broadcasted_iota(jnp.int32, (1, rows), 1)
+    for h in range(group):
+        at = slice(h * rows, (h + 1) * rows)
+        scaled = blend[:, at] / jnp.maximum(total[:, at], 1.0)
+        scaled = jnp.where(row_lane < own_len, scaled, 0.0)
+        attention[s, :, h * HEAD : (h + 1) * HEAD] = jnp.transpose(scaled).astype(BF16)
+
+    att_copy = pltpu.make_async_remote_copy(
+        src_ref=attention.at[1],
+        dst_ref=attention.at[1],
+        send_sem=att_sem.at[0],
+        recv_sem=att_sem.at[1],
+        device_id={"section": 1 - s},
+        device_id_type=MESH,
+    )
+
+    def term_own(j):
+        return pltpu.make_async_remote_copy(
+            src_ref=terms.at[j],
+            dst_ref=own_terms.at[j],
+            send_sem=term_own_send.at[j],
+            recv_sem=term_own_recv.at[j],
+            device_id={"section": 1 - s},
+            device_id_type=MESH,
+        )
+
+    def term_far(j):
+        return pltpu.make_async_remote_copy(
+            src_ref=terms.at[j],
+            dst_ref=far_terms.at[j],
+            send_sem=term_far_send.at[j],
+            recv_sem=term_far_recv.at[j],
+            device_id={"section": 1 - s, "tp": 1 - p},
+            device_id_type=MESH,
+        )
+
+    def hid(j):
+        return pltpu.make_async_remote_copy(
+            src_ref=hidden_buf.at[j],
+            dst_ref=hidden_out.at[:, pl.ds(pl.multiple_of(j * CHUNK, CHUNK), CHUNK)],
+            send_sem=hid_send.at[j],
+            recv_sem=hid_recv.at[j],
+            device_id={"section": 1 - s},
+            device_id_type=MESH,
+        )
+
+    def each(count, act):
+        def one(j, carry):
+            act(j)
+            return carry
+
+        lax.fori_loop(0, count, one, 0)
+
+    @pl.when(s == 0)
+    def _():
+        weights_copy.wait()
+        att_copy.wait_recv()
+
+        def project(j, carry):
+            at = pl.ds(pl.multiple_of(j * CHUNK, CHUNK), CHUNK)
+            both = jnp.concatenate([attention[0], attention[1]], axis=1)
+            terms[j] = nn(both, weights[:, at]).astype(BF16)
+            term_far(j).start()
+            term_own(j).start()
+            return carry
+
+        lax.fori_loop(0, chunks, project, 0)
+        head_out[:, 0:wide] = attention[0]
+        head_out[:, wide : 2 * wide] = attention[1]
+        each(chunks, lambda j: term_far(j).wait_send())
+        each(chunks, lambda j: term_own(j).wait_send())
+        key_copy.wait_send()
+        query_copy.wait_send()
+        each(chunks_half, lambda j: hid(j).wait_recv())
+
+    @pl.when(s == 1)
+    def _():
+        att_copy.start()
+        heads = 2 * group
+        row_col = lax.broadcasted_iota(jnp.int32, (rows, 1), 0)
+        valid_col = row_col < own_len
+        r = lax.broadcasted_iota(jnp.int32, (rows, rows), 0)
+        t = lax.broadcasted_iota(jnp.int32, (rows, rows), 1)
+        lower = jnp.where(r >= t, 1.0, 0.0)
+        upper = jnp.where(r <= t, 1.0, 0.0)
+        cum = jnp.dot(
+            lower,
+            jnp.where(valid_col, decay[...], 0.0),
+            precision=lax.Precision.HIGHEST,
+            preferred_element_type=F32,
+        )
+        cum_t = jnp.dot(
+            jnp.where(row_lane < own_len, decay_t[...], 0.0),
+            upper,
+            precision=lax.Precision.HIGHEST,
+            preferred_element_type=F32,
+        )
+        last = cum[rows - 1 : rows, :]
+        rest[...] = jnp.exp(last - cum)
+        for g in range(2):
+            masked = jnp.where(valid_col, keys[:, g * HEAD : (g + 1) * HEAD].astype(F32), 0.0)
+            keys_t[g] = jnp.transpose(masked).astype(BF16)
+        for h in range(heads):
+            at = slice(h * HEAD, (h + 1) * HEAD)
+            col = cum[:, h : h + 1]
+            row = cum_t[h : h + 1, :]
+            query = queries[:, at]
+            damping = jnp.where(r >= t, jnp.exp(jnp.minimum(col - row, 0.0)), 0.0)
+            damped[h] = (nn(query, keys_t[h // group]) * damping).astype(BF16)
+            faded[:, at] = (query.astype(F32) * jnp.exp(col)).astype(BF16)
+            sum_row = jnp.broadcast_to(last[:, h : h + 1], (PAD, HEAD))
+            high = sum_row.astype(BF16)
+            low = (sum_row - high.astype(F32)).astype(BF16)
+            states[0, HEAD : HEAD + PAD, at] = high
+            states[0, HEAD + PAD : HEAD + 2 * PAD, at] = low
+        values_sum[...] = jnp.zeros_like(values_sum)
+        square_sum[...] = jnp.zeros_like(square_sum)
+        weights_copy.wait()
+        residual_copy.wait()
+        residual_recv.wait_recv()
+
+        def collect(j, carry):
+            side = j // chunks_half
+            col = j - side * chunks_half
+            here = pl.ds(pl.multiple_of(col * CHUNK, CHUNK), CHUNK)
+            at = pl.ds(pl.multiple_of(j * CHUNK, CHUNK), CHUNK)
+            term_own(j).wait_recv()
+            term_far(j).wait_recv()
+            summed = residuals[side, :, here].astype(F32) + (
+                own_terms[j].astype(F32) + far_terms[j].astype(F32)
+            )
+            narrow = summed.astype(BF16)
+
+            @pl.when(side == p)
+            def _():
+                hidden_buf[col] = narrow
+                hidden_out[:, here] = narrow
+                hid(col).start()
+
+            rounded = narrow.astype(F32)
+            square_sum[...] += jnp.sum(rounded * rounded, axis=1, keepdims=True)
+            ready = (rounded * gain[:, at].astype(F32)).astype(BF16)
+            values_sum[...] += nt(ready, weights[:, at])
+            return carry
+
+        lax.fori_loop(0, chunks, collect, 0)
+        scale = lax.rsqrt(square_sum[...] * (1.0 / (2 * half)) + 1e-05)
+        values[...] = (values_sum[...] * scale).astype(BF16)
+        for h in range(heads):
+            at = slice(h * HEAD, (h + 1) * HEAD)
+            weighted = (values[:, at].astype(F32) * rest[:, h : h + 1]).astype(BF16)
+            states[0, 0:HEAD, at] = nn(keys_t[h // group], weighted).astype(BF16)
+        send_own(states, state_send, state_forward, state_recv)
+        for h in range(heads):
+            at = slice(h * HEAD, (h + 1) * HEAD)
+            mixed[:, at] = nn(damped[h], values[:, at])
+        incoming[...] = jnp.zeros_like(incoming)
+        passed[...] = jnp.zeros_like(passed)
+
+        def join(slot):
+            incoming[...] += states[slot, 0:HEAD, :].astype(F32) * jnp.exp(passed[0:1, :])
+            passed[...] += states[slot, HEAD : HEAD + PAD, :].astype(F32) + states[
+                slot, HEAD + PAD : HEAD + 2 * PAD, :
+            ].astype(F32)
+
+        def join_pair(k, carry):
+            arrival(states, state_send, state_recv, 2 * k).wait_recv()
+            forward(states, state_forward, state_recv, k).start()
+            arrival(states, state_send, state_recv, 2 * k - 1).wait_recv()
+            join(2 * k - 1)
+            join(2 * k)
+            return carry
+
+        lax.fori_loop(1, before + 1, join_pair, 0)
+
+        @pl.when(odd == 1)
+        def _():
+            arrival(states, state_send, state_recv, c).wait_recv()
+            join(c)
+
+        spike_copy.wait()
+        for h in range(heads):
+            at = slice(h * HEAD, (h + 1) * HEAD)
+            both = mixed[:, at] + nn(faded[:, at], incoming[:, at].astype(BF16))
+            scaled = both * lax.rsqrt(jnp.mean(both * both, axis=1, keepdims=True) + 1e-05)
+            gated = scaled * (spike_buf[:, at].astype(F32) * thresholds[:, at])
+            head_out[:, at] = jnp.where(valid_col, gated, 0.0).astype(BF16)
+        sent_own(states, state_send, state_forward, state_recv)
+        each(chunks_half, lambda j: hid(j).wait_send())
+        residual_send.wait_send()
+        att_copy.wait_send()
+
+    sent_own(kv, kv_send, kv_forward, kv_recv)
+
+
+def fused(
+    residual,
+    queries,
+    keys,
+    window_values,
+    mixing,
+    norm_gain,
+    log_decay,
+    spike_counts,
+    thresholds,
+    lengths,
+):
+    n = lax.axis_size("ctx")
+    rows, half = residual.shape
+    width = queries.shape[2]
+    heads = width // HEAD
+    chunks = 2 * half // CHUNK
+    dma = pltpu.SemaphoreType.DMA
+    whole = pl.BlockSpec(memory_space=pltpu.VMEM)
+    away = pl.BlockSpec(memory_space=pl.ANY)
+    head_outputs, hidden = pl.pallas_call(
+        functools.partial(kernel, n),
+        out_shape=(
+            jax.ShapeDtypeStruct((rows, width), BF16),
+            jax.ShapeDtypeStruct((rows, half), BF16),
+        ),
+        in_specs=[
+            away,
+            whole,
+            whole,
+            whole,
+            away,
+            whole,
+            whole,
+            whole,
+            away,
+            whole,
+            pl.BlockSpec(memory_space=pltpu.SMEM),
+        ],
+        out_specs=(whole, whole),
+        scratch_shapes=[
+            pltpu.VMEM(mixing.shape[1:], BF16),
+            pltpu.VMEM((rows, width), jnp.int32),
+            pltpu.VMEM((n, 2 * rows, HEAD), BF16),
+            pltpu.VMEM((rows, width // 2), BF16),
+            pltpu.VMEM((4 * rows, HEAD), BF16),
+            pltpu.VMEM((1, 4 * rows), F32),
+            pltpu.VMEM((1, 4 * rows), F32),
+            pltpu.VMEM((HEAD, 4 * rows), F32),
+            pltpu.VMEM((2, rows, width // 2), BF16),
+            pltpu.VMEM((chunks, rows, CHUNK), BF16),
+            pltpu.VMEM((chunks, rows, CHUNK), BF16),
+            pltpu.VMEM((chunks, rows, CHUNK), BF16),
+            pltpu.VMEM((2, rows, half), BF16),
+            pltpu.VMEM((chunks // 2, rows, CHUNK), BF16),
+            pltpu.VMEM((rows, width), F32),
+            pltpu.VMEM((rows, 1), F32),
+            pltpu.VMEM((heads, rows, rows), BF16),
+            pltpu.VMEM((rows, width), BF16),
+            pltpu.VMEM((rows, heads), F32),
+            pltpu.VMEM((2, HEAD, rows), BF16),
+            pltpu.VMEM((rows, width), BF16),
+            pltpu.VMEM((n, HEAD + 2 * PAD, width), BF16),
+            pltpu.VMEM((HEAD, width), F32),
+            pltpu.VMEM((PAD, width), F32),
+            pltpu.VMEM((rows, width), F32),
+            dma,
+            dma,
+            dma((3,)),
+            dma((2,)),
+            dma((2,)),
+            dma((n // 2,)),
+            dma((n,)),
+            dma((n // 2,)),
+            dma((2,)),
+            dma((chunks,)),
+            dma((chunks,)),
+            dma((chunks,)),
+            dma((chunks,)),
+            dma((chunks // 2,)),
+            dma((chunks // 2,)),
+            dma((n // 2,)),
+            dma((n,)),
+            dma((n // 2,)),
+        ],
+        compiler_params=pltpu.CompilerParams(
+            collective_id=0, has_side_effects=True, vmem_limit_bytes=56 * 1024 * 1024
+        ),
+    )(
+        residual,
+        queries[0],
+        keys[0],
+        window_values,
+        mixing[0],
+        norm_gain.reshape(1, -1),
+        log_decay,
+        log_decay.T,
+        spike_counts,
+        thresholds.reshape(1, -1),
+        lengths,
+    )
+    return (head_outputs[None], hidden)
+
+
+def chosen(*arrays):
+    residual, queries, keys = arrays[:3]
+    shards = lax.axis_size("ctx")
+    rows = residual.shape[0]
+    fits = (
+        lax.axis_size("tp") == 2
+        and lax.axis_size("section") == 2
+        and keys.shape[2] == 2 * HEAD
+        and queries.shape[2] == 8 * HEAD
+        and rows == 2 * HEAD
+        and residual.shape[1] % CHUNK == 0
+        and shards % 2 == 0
+        and shards * rows <= WINDOW
+    )
+    return fused(*arrays) if fits else body(*arrays)
+
+
 def solution(mesh):
     return jax.shard_map(
-        body,
+        chosen,
         mesh=mesh,
         in_specs=(
             P("ctx", "tp"),

time: 350 us -> 80.9 us (0.23)
  waiting for transfers between devices: 244 us -> 0 us
  Pallas kernels: 0 us -> 71.9 us
  local copies, waits for them, and re-layouts: 31.5 us -> 6.82 us
  starting transfers between devices: 21.2 us -> 0 us
  between operations: 14.2 us -> 0.64 us
  blocking collectives: 12.5 us -> 0 us
  other arithmetic: 12 us -> 0 us
  matrix products: 11.4 us -> 0 us
    reduce_scatter x1 -> x0, waiting for transfers between devices: 157 us -> none  [body(): lax.psum_scatter(projected.astype(jnp.bfloat16), 'tp', scatter_dimension=...]
    pallas_call x0 -> x1, Pallas kernels: none -> 71.9 us  [fused(): pl.pallas_call(functools.partial(kernel, n), out_shape=(jax.ShapeDtypeStr...]
    all_gather x2 -> x0, waiting for transfers between devices: 62.4 us -> none  [the longest x1 33.9 us: entering(): lax.all_gather(a.astype(kind), axis)]
    ppermute x17 -> x0, waiting for transfers between devices: 25 us -> none  [passed_along(): return lax.ppermute(x, axis, pairs)]
    ppermute x17 -> x0, starting transfers between devices: 21.1 us -> none  [passed_along(): return lax.ppermute(x, axis, pairs)]
    all_gather x1 -> x0, blocking collectives: 12.5 us -> none  [entering(): lax.all_gather(a.astype(kind), axis)]
    dot_general x5 -> x0, matrix products: 11.4 us -> none  [the longest x1 6.56 us: linear_prepare(): lax.dot_general(normed, mixing[0], (((1,), (1,)), ((), ())), preferred_el...]
    unnamed x49 -> x3, local copies, waits for them, and re-layouts: 12.9 us -> 5.51 us
  transfers between devices with their start and end apart: 20 -> 0, of which waited for: 9 -> 0; matrix products, arithmetic and copies ran while one was open for 4% -> 0% of each run, Pallas kernels for 0% -> 0%
where the time goes in v1:
time: 80.9 us; the launch traced here: 79.3 us
  Pallas kernels  71.9 us (89%)
  local copies, waits for them, and re-layouts  6.82 us (8%)
    pallas_call x1, Pallas kernels, fused(): pl.pallas_call(functools.partial(kernel, n), out_shape=(jax.ShapeDtypeStr...  71.9 us
    unnamed x3, local copies, waits for them, and re-layouts  5.51 us

profile of v1, /device:TPU:25, one launch (start us, length us, event | category | flops | bytes accessed | tf_op | source)
XLA Modules:
  0.0 79.3 jit_solution(1957721961735356164)
XLA Ops:
  0.6 1.3 %reshape.10.gain = bf16[1,3584]{1,0:T(2,128)(2,1)} reshape(bf16[3584]{0:T(1024)(128)(2,1)} %param.15) | data formatting | bytes 14336 | tf_op jit(solution)/shard_map/reshape | solution.py:804
  1.9 1.5 %copy.12.decay = f32[256,8]{1,0:T(8,128)} copy(f32[256,8]{0,1:T(8,128)} %param.16) | data formatting | bytes 16384 | tf_op args[6]
  3.4 71.9 %shard_map.113 = (bf16[256,1024]{1,0:T(8,128)(2,1)}, bf16[256,1792]{1,0:T(8,128)(2,1)}) custom-call(bf16[256,1792]{1,0:T(8,128)(2,1)} %residual.1, bf16[256,1024]{1,0:T(8,128)(2,1)} %bitcast.7, bf16[256,256]{1,0:T(8,128)(2,1)} %bitcast.9, bf16[256,256]{1,0:T(8,128)(2,1)} %window_values.1, bf16[1024,3584]{1,0:T(8,128)(2,1)} %bitcast.6, ...), custom_call_target="tpu_custom_call" | custom-call | tf_op jit(solution)/shard_map/pallas_call | solution.py:730
  75.3 1.9 %copy.15 = bf16[1,256,1024]{2,1,0:T(8,128)(2,1)} copy(bf16[1,256,1024]{2,1,0:T(8,128)(2,1)} %bitcast.8) | data formatting | bytes 1048576
  77.2 2.2 %copy.16 = bf16[256,1792]{1,0:T(8,128)(2,1)} copy(bf16[256,1792]{1,0:T(8,128)(2,1)} %get-tuple-element.9) | data formatting | bytes 1835008

commit v2 on v1

--- a/solution.py
+++ b/solution.py
@@ -253,7 +253,6 @@
     window_values,
     mixing,
     gain,
-    decay,
     decay_t,
     spikes,
     thresholds,
@@ -282,9 +281,12 @@
     keys_t,
     values,
     states,
+    fresh,
     incoming,
     passed,
     mixed,
+    gain_row,
+    decay_wide,
     weights_sem,
     spike_sem,
     res_sem,
@@ -300,9 +302,10 @@
     term_far_recv,
     hid_send,
     hid_recv,
+    swap_send,
+    swap_recv,
     state_send,
     state_recv,
-    state_forward,
 ):
     c = lax.axis_index("ctx")
     s = lax.axis_index("section")
@@ -399,68 +402,46 @@
         spike_copy.start()
         key_copy.wait_recv()
 
-    def direct(buf, send, recv, k):
+    def along(k):
         return pltpu.make_async_remote_copy(
-            src_ref=buf.at[0],
-            dst_ref=buf.at[2 * k],
-            send_sem=send.at[k],
-            recv_sem=recv.at[2 * k],
-            device_id={"ctx": lax.rem(c + 2 * k, n)},
+            src_ref=kv.at[2 * k],
+            dst_ref=kv.at[2 * k + 2],
+            send_sem=kv_send.at[k],
+            recv_sem=kv_recv.at[2 * k + 2],
+            device_id={"ctx": lax.rem(c + 2, n)},
             device_id_type=MESH,
         )
 
-    def forward(buf, send, recv, k):
+    def across(k):
         return pltpu.make_async_remote_copy(
-            src_ref=buf.at[2 * k],
-            dst_ref=buf.at[2 * k + step_to],
-            send_sem=send.at[k],
-            recv_sem=recv.at[2 * k + step_to],
+            src_ref=kv.at[2 * k],
+            dst_ref=kv.at[2 * k + step_to],
+            send_sem=kv_forward.at[k],
+            recv_sem=kv_recv.at[2 * k + step_to],
             device_id={"ctx": partner},
             device_id_type=MESH,
         )
 
-    def arrival(buf, send, recv, slot):
+    def arrival(slot):
         return pltpu.make_async_remote_copy(
-            src_ref=buf.at[slot],
-            dst_ref=buf.at[slot],
-            send_sem=send.at[0],
-            recv_sem=recv.at[slot],
+            src_ref=kv.at[slot],
+            dst_ref=kv.at[slot],
+            send_sem=kv_send.at[0],
+            recv_sem=kv_recv.at[slot],
             device_id={"ctx": partner},
             device_id_type=MESH,
         )
 
-    later = (n - 1 - c) // 2
     before = c // 2
-
-    def send_own(buf, send, forward_sem, recv):
-        @pl.when(odd == 0)
-        def _():
-            forward(buf, forward_sem, recv, 0).start()
-
-        def one(k, carry):
-            direct(buf, send, recv, k).start()
-            return carry
-
-        lax.fori_loop(1, later + 1, one, 0)
-
-    def sent_own(buf, send, forward_sem, recv):
-        @pl.when(odd == 0)
-        def _():
-            forward(buf, forward_sem, recv, 0).wait_send()
-
-        def one(k, carry):
-            direct(buf, send, recv, k).wait_send()
-            return carry
-
-        lax.fori_loop(1, later + 1, one, 0)
-
-        def two(k, carry):
-            forward(buf, forward_sem, recv, k).wait_send()
-            return carry
-
-        lax.fori_loop(1, before + 1, two, 0)
-
-    send_own(kv, kv_send, kv_forward, kv_recv)
+    pairs = n // 2
+
+    @pl.when(c + 2 < n)
+    def _():
+        along(0).start()
+
+    @pl.when(odd == 0)
+    def _():
+        across(0).start()
 
     @pl.when(s == 1)
     def _():
@@ -498,18 +479,23 @@
     attend(0, True)
 
     def attend_pair(k, carry):
-        arrival(kv, kv_send, kv_recv, 2 * k).wait_recv()
-        forward(kv, kv_forward, kv_recv, k).start()
+        arrival(2 * k).wait_recv()
+
+        @pl.when(c + 2 < n)
+        def _():
+            along(k).start()
+
+        across(k).start()
+        arrival(2 * k - 1).wait_recv()
+        attend(2 * k - 1, False)
         attend(2 * k, False)
-        arrival(kv, kv_send, kv_recv, 2 * k - 1).wait_recv()
-        attend(2 * k - 1, False)
         return carry
 
     lax.fori_loop(1, before + 1, attend_pair, 0)
 
     @pl.when(odd == 1)
     def _():
-        arrival(kv, kv_send, kv_recv, c).wait_recv()
+        arrival(c).wait_recv()
         attend(c, False)
 
     row_lane = lax.broadcasted_iota(jnp.int32, (1, rows), 1)
@@ -595,20 +581,14 @@
         valid_col = row_col < own_len
         r = lax.broadcasted_iota(jnp.int32, (rows, rows), 0)
         t = lax.broadcasted_iota(jnp.int32, (rows, rows), 1)
-        lower = jnp.where(r >= t, 1.0, 0.0)
         upper = jnp.where(r <= t, 1.0, 0.0)
-        cum = jnp.dot(
-            lower,
-            jnp.where(valid_col, decay[...], 0.0),
-            precision=lax.Precision.HIGHEST,
-            preferred_element_type=F32,
-        )
+        decay_wide[...] = jnp.zeros_like(decay_wide)
+        decay_wide[0:heads, :] = jnp.where(row_lane < own_len, decay_t[...], 0.0)
         cum_t = jnp.dot(
-            jnp.where(row_lane < own_len, decay_t[...], 0.0),
-            upper,
-            precision=lax.Precision.HIGHEST,
-            preferred_element_type=F32,
-        )
+            decay_wide[...], upper, precision=lax.Precision.HIGHEST, preferred_element_type=F32
+        )
+        cum = jnp.transpose(cum_t)
+        gain_row[...] = gain[...].astype(F32).reshape(1, 2 * half)
         last = cum[rows - 1 : rows, :]
         rest[...] = jnp.exp(last - cum)
         for g in range(2):
@@ -624,9 +604,13 @@
             faded[:, at] = (query.astype(F32) * jnp.exp(col)).astype(BF16)
             sum_row = jnp.broadcast_to(last[:, h : h + 1], (PAD, HEAD))
             high = sum_row.astype(BF16)
-            low = (sum_row - high.astype(F32)).astype(BF16)
-            states[0, HEAD : HEAD + PAD, at] = high
-            states[0, HEAD + PAD : HEAD + 2 * PAD, at] = low
+            low = sum_row - high.astype(F32)
+            in_group = slice((h % group) * HEAD, (h % group + 1) * HEAD)
+            states[0, h // group, HEAD : HEAD + PAD, in_group] = jnp.where(
+                lax.broadcasted_iota(jnp.int32, (PAD, HEAD), 0) < PAD // 2,
+                high.astype(F32),
+                low,
+            ).astype(BF16)
         values_sum[...] = jnp.zeros_like(values_sum)
         square_sum[...] = jnp.zeros_like(square_sum)
         weights_copy.wait()
@@ -653,58 +637,156 @@
 
             rounded = narrow.astype(F32)
             square_sum[...] += jnp.sum(rounded * rounded, axis=1, keepdims=True)
-            ready = (rounded * gain[:, at].astype(F32)).astype(BF16)
+            ready = (rounded * gain_row[:, at]).astype(BF16)
             values_sum[...] += nt(ready, weights[:, at])
             return carry
 
         lax.fori_loop(0, chunks, collect, 0)
         scale = lax.rsqrt(square_sum[...] * (1.0 / (2 * half)) + 1e-05)
         values[...] = (values_sum[...] * scale).astype(BF16)
-        for h in range(heads):
-            at = slice(h * HEAD, (h + 1) * HEAD)
-            weighted = (values[:, at].astype(F32) * rest[:, h : h + 1]).astype(BF16)
-            states[0, 0:HEAD, at] = nn(keys_t[h // group], weighted).astype(BF16)
-        send_own(states, state_send, state_forward, state_recv)
+        def swap(g):
+            return pltpu.make_async_remote_copy(
+                src_ref=states.at[0, g],
+                dst_ref=states.at[1, g],
+                send_sem=swap_send.at[g],
+                recv_sem=swap_recv.at[g],
+                device_id={"ctx": partner},
+                device_id_type=MESH,
+            )
+
+        def onward(k, g):
+            return pltpu.make_async_remote_copy(
+                src_ref=states.at[2, g],
+                dst_ref=states.at[2 + k, g],
+                send_sem=state_send.at[k, g],
+                recv_sem=state_recv.at[k, g],
+                device_id={"ctx": lax.rem(c + 2 * k, n)},
+                device_id_type=MESH,
+            )
+
+        def sum_of(slot, g):
+            rows_of = states[slot, g, HEAD : HEAD + PAD, :].astype(F32)
+            return rows_of[0:1, :] + rows_of[PAD // 2 : PAD // 2 + 1, :]
+
+        here_later = pairs - 1 - before
+        swap_out = (odd == 0) | (here_later > 0)
+        swap_in = (odd == 1) | (here_later > 0)
+        for g in range(2):
+            for h in range(g * group, (g + 1) * group):
+                at = slice(h * HEAD, (h + 1) * HEAD)
+                weighted = (values[:, at].astype(F32) * rest[:, h : h + 1]).astype(BF16)
+                fresh[:, at] = nn(keys_t[g], weighted)
+                in_group = slice((h % group) * HEAD, (h % group + 1) * HEAD)
+                states[0, g, 0:HEAD, in_group] = fresh[:, at].astype(BF16)
+
+            @pl.when(swap_out)
+            def _():
+                swap(g).start()
+
         for h in range(heads):
             at = slice(h * HEAD, (h + 1) * HEAD)
             mixed[:, at] = nn(damped[h], values[:, at])
-        incoming[...] = jnp.zeros_like(incoming)
-        passed[...] = jnp.zeros_like(passed)
-
-        def join(slot):
-            incoming[...] += states[slot, 0:HEAD, :].astype(F32) * jnp.exp(passed[0:1, :])
-            passed[...] += states[slot, HEAD : HEAD + PAD, :].astype(F32) + states[
-                slot, HEAD + PAD : HEAD + 2 * PAD, :
-            ].astype(F32)
-
-        def join_pair(k, carry):
-            arrival(states, state_send, state_recv, 2 * k).wait_recv()
-            forward(states, state_forward, state_recv, k).start()
-            arrival(states, state_send, state_recv, 2 * k - 1).wait_recv()
-            join(2 * k - 1)
-            join(2 * k)
-            return carry
-
-        lax.fori_loop(1, before + 1, join_pair, 0)
-
-        @pl.when(odd == 1)
-        def _():
-            arrival(states, state_send, state_recv, c).wait_recv()
-            join(c)
+
+        for g in range(2):
+            at = slice(g * wide, (g + 1) * wide)
+
+            @pl.when(swap_in)
+            def _():
+                swap(g).wait_recv()
+
+            @pl.when(here_later > 0)
+            def _():
+                own_sum = sum_of(0, g)
+                other_sum = sum_of(1, g)
+                second = jnp.where(odd == 1, own_sum, other_sum)
+                own = fresh[:, at]
+                other = states[1, g, 0:HEAD, :].astype(F32)
+                first_part = jnp.where(odd == 1, other, own)
+                second_part = jnp.where(odd == 1, own, other)
+                states[2, g, 0:HEAD, :] = (first_part * jnp.exp(second) + second_part).astype(BF16)
+                both_sum = jnp.broadcast_to(own_sum + other_sum, (PAD, wide))
+                high = both_sum.astype(BF16).astype(F32)
+                states[2, g, HEAD : HEAD + PAD, :] = jnp.where(
+                    lax.broadcasted_iota(jnp.int32, (PAD, wide), 0) < PAD // 2,
+                    high,
+                    both_sum - high,
+                ).astype(BF16)
+
+                def send_on(k, carry):
+                    onward(k, g).start()
+                    return carry
+
+                lax.fori_loop(1, here_later + 1, send_on, 0)
 
         spike_copy.wait()
-        for h in range(heads):
-            at = slice(h * HEAD, (h + 1) * HEAD)
-            both = mixed[:, at] + nn(faded[:, at], incoming[:, at].astype(BF16))
-            scaled = both * lax.rsqrt(jnp.mean(both * both, axis=1, keepdims=True) + 1e-05)
-            gated = scaled * (spike_buf[:, at].astype(F32) * thresholds[:, at])
-            head_out[:, at] = jnp.where(valid_col, gated, 0.0).astype(BF16)
-        sent_own(states, state_send, state_forward, state_recv)
+        for g in range(2):
+            at = slice(g * wide, (g + 1) * wide)
+
+            @pl.when(odd == 1)
+            def _():
+                incoming[:, at] = states[1, g, 0:HEAD, :].astype(F32)
+                passed[:, at] = sum_of(1, g)
+
+            @pl.when(odd == 0)
+            def _():
+                incoming[:, at] = jnp.zeros((HEAD, wide), F32)
+                passed[:, at] = jnp.zeros((1, wide), F32)
+
+            def join(k, carry):
+                onward(k, g).wait_recv()
+                incoming[:, at] += states[2 + k, g, 0:HEAD, :].astype(F32) * jnp.exp(passed[:, at])
+                passed[:, at] += sum_of(2 + k, g)
+                return carry
+
+            lax.fori_loop(1, before + 1, join, 0)
+            for h in range(g * group, (g + 1) * group):
+                at = slice(h * HEAD, (h + 1) * HEAD)
+                both = mixed[:, at] + nn(faded[:, at], incoming[:, at].astype(BF16))
+                scaled = both * lax.rsqrt(jnp.mean(both * both, axis=1, keepdims=True) + 1e-05)
+                gated = scaled * (spike_buf[:, at].astype(F32) * thresholds[:, at])
+                head_out[:, at] = jnp.where(valid_col, gated, 0.0).astype(BF16)
+
+        for g in range(2):
+
+            @pl.when(swap_out)
+            def _():
+                swap(g).wait_send()
+
+            def sent_on(k, carry):
+                onward(k, g).wait_send()
+                return carry
+
+            lax.fori_loop(1, here_later + 1, sent_on, 0)
         each(chunks_half, lambda j: hid(j).wait_send())
         residual_send.wait_send()
         att_copy.wait_send()
 
-    sent_own(kv, kv_send, kv_forward, kv_recv)
+    def along_done(k, carry):
+        along(k).wait_send()
+        return carry
+
+    @pl.when(c + 2 < n)
+    def _():
+        lax.fori_loop(0, before + 1, along_done, 0)
+
+    @pl.when(odd == 0)
+    def _():
+        across(0).wait_send()
+
+    def across_done(k, carry):
+        across(k).wait_send()
+        return carry
+
+    lax.fori_loop(1, before + 1, across_done, 0)
+
+
+def handed_on(a, b, a_out, b_out, a_sem, b_sem):
+    one = pltpu.make_async_copy(a, a_out, a_sem)
+    two = pltpu.make_async_copy(b, b_out, b_sem)
+    one.start()
+    two.start()
+    one.wait()
+    two.wait()
 
 
 def fused(
@@ -741,7 +823,6 @@
             away,
             whole,
             whole,
-            whole,
             away,
             whole,
             pl.BlockSpec(memory_space=pltpu.SMEM),
@@ -766,13 +847,16 @@
             pltpu.VMEM((rows, 1), F32),
             pltpu.VMEM((heads, rows, rows), BF16),
             pltpu.VMEM((rows, width), BF16),
-            pltpu.VMEM((rows, heads), F32),
+            pltpu.VMEM((rows, HEAD), F32),
             pltpu.VMEM((2, HEAD, rows), BF16),
             pltpu.VMEM((rows, width), BF16),
-            pltpu.VMEM((n, HEAD + 2 * PAD, width), BF16),
+            pltpu.VMEM((n // 2 + 2, 2, HEAD + PAD, width // 2), BF16),
             pltpu.VMEM((HEAD, width), F32),
-            pltpu.VMEM((PAD, width), F32),
+            pltpu.VMEM((HEAD, width), F32),
+            pltpu.VMEM((1, width), F32),
             pltpu.VMEM((rows, width), F32),
+            pltpu.VMEM((1, 2 * half), F32),
+            pltpu.VMEM((HEAD, rows), F32),
             dma,
             dma,
             dma((3,)),
@@ -788,9 +872,10 @@
             dma((chunks,)),
             dma((chunks // 2,)),
             dma((chunks // 2,)),
-            dma((n // 2,)),
-            dma((n,)),
-            dma((n // 2,)),
+            dma((2,)),
+            dma((2,)),
+            dma((n // 2, 2)),
+            dma((n // 2, 2)),
         ],
         compiler_params=pltpu.CompilerParams(
             collective_id=0, has_side_effects=True, vmem_limit_bytes=56 * 1024 * 1024
@@ -801,13 +886,23 @@
         keys[0],
         window_values,
         mixing[0],
-        norm_gain.reshape(1, -1),
-        log_decay,
+        norm_gain,
         log_decay.T,
         spike_counts,
         thresholds.reshape(1, -1),
         lengths,
     )
+    head_outputs, hidden = pl.pallas_call(
+        handed_on,
+        out_shape=(
+            jax.ShapeDtypeStruct((rows, width), BF16),
+            jax.ShapeDtypeStruct((rows, half), BF16),
+        ),
+        in_specs=[away, away],
+        out_specs=(away, away),
+        scratch_shapes=[dma, dma],
+        compiler_params=pltpu.CompilerParams(vmem_limit_bytes=60 * 1024 * 1024),
+    )(head_outputs, hidden)
     return (head_outputs[None], hidden)
 
 

time: 80.9 us -> 106 us (1.31); the launches traced: 79.3 us -> 106 us
  Pallas kernels: 71.9 us -> 105 us
  local copies, waits for them, and re-layouts: 6.82 us -> 0 us
    pallas_call x0 -> x1, Pallas kernels: none -> 44.8 us  [fused(): pl.pallas_call(handed_on, out_shape=(jax.ShapeDtypeStruct((rows, width),...]
    pallas_call x1, Pallas kernels: 71.9 us -> 60.6 us  [fused(): pl.pallas_call(functools.partial(kernel, n), out_shape=(jax.ShapeDtypeStr...]
    unnamed x3 -> x0, local copies, waits for them, and re-layouts: 5.51 us -> none
    reshape x1 -> x0, local copies, waits for them, and re-layouts: 1.31 us -> none  [fused(): norm_gain.reshape(1, -1)]
where the time goes in v2:
time: 106 us
  Pallas kernels  105 us (99%)
    pallas_call x1, Pallas kernels, fused(): pl.pallas_call(functools.partial(kernel, n), out_shape=(jax.ShapeDtypeStr...  60.6 us
    pallas_call x1, Pallas kernels, fused(): pl.pallas_call(handed_on, out_shape=(jax.ShapeDtypeStruct((rows, width),...  44.8 us

profile of v2, /device:TPU:25, one launch (start us, length us, event | category | flops | bytes accessed | tf_op | source)
XLA Modules:
  0.0 106.1 jit_solution(9265818426721679486)
XLA Ops:
  0.6 60.6 %shard_map.113 = (bf16[256,1024]{1,0:T(8,128)(2,1)}, bf16[256,1792]{1,0:T(8,128)(2,1)}) custom-call(bf16[256,1792]{1,0:T(8,128)(2,1)} %residual.1, bf16[256,1024]{1,0:T(8,128)(2,1)} %bitcast.7, bf16[256,256]{1,0:T(8,128)(2,1)} %bitcast.8, bf16[256,256]{1,0:T(8,128)(2,1)} %window_values.1, bf16[1024,3584]{1,0:T(8,128)(2,1)} %bitcast.6, bf16[3584]{0:T(1024)(128)(2,1)} %gain.1, ...), custom_call_target="tpu_custom_call" | custom-call | tf_op jit(solution)/shard_map/pallas_call | solution.py:812
  61.3 44.8 %shard_map.114 = (bf16[256,1024]{1,0:T(8,128)(2,1)}, bf16[256,1792]{1,0:T(8,128)(2,1)}) custom-call(bf16[256,1024]{1,0:T(8,128)(2,1)} %get-tuple-element.6.a, bf16[256,1792]{1,0:T(8,128)(2,1)} %get-tuple-element.7.b), custom_call_target="tpu_custom_call" | custom-call | tf_op jit(solution)/shard_map/pallas_call | solution.py:895

commit v3 on v2

--- a/solution.py
+++ b/solution.py
@@ -231,6 +231,7 @@
 BF16 = jnp.bfloat16
 CHUNK = 256
 PAD = 16
+PIECES = 4
 
 
 def nt(a, b):
@@ -560,14 +561,20 @@
             at = pl.ds(pl.multiple_of(j * CHUNK, CHUNK), CHUNK)
             both = jnp.concatenate([attention[0], attention[1]], axis=1)
             terms[j] = nn(both, weights[:, at]).astype(BF16)
+            term_own(j).start()
+
+            @pl.when(j >= 2)
+            def _():
+                term_far(j - 2).wait_send()
+
             term_far(j).start()
-            term_own(j).start()
             return carry
 
         lax.fori_loop(0, chunks, project, 0)
         head_out[:, 0:wide] = attention[0]
         head_out[:, wide : 2 * wide] = attention[1]
-        each(chunks, lambda j: term_far(j).wait_send())
+        term_far(chunks - 2).wait_send()
+        term_far(chunks - 1).wait_send()
         each(chunks, lambda j: term_own(j).wait_send())
         key_copy.wait_send()
         query_copy.wait_send()
@@ -780,13 +787,28 @@
     lax.fori_loop(1, before + 1, across_done, 0)
 
 
-def handed_on(a, b, a_out, b_out, a_sem, b_sem):
-    one = pltpu.make_async_copy(a, a_out, a_sem)
-    two = pltpu.make_async_copy(b, b_out, b_sem)
-    one.start()
-    two.start()
-    one.wait()
-    two.wait()
+def handed_on(a, b, a_out, b_out, a_buf, b_buf, in_sem, out_sem):
+    step = a.shape[0] // PIECES
+
+    def copies(i):
+        at = slice(i * step, (i + 1) * step)
+        return (
+            pltpu.make_async_copy(b.at[at], b_buf.at[at], in_sem.at[0, i]),
+            pltpu.make_async_copy(a.at[at], a_buf.at[at], in_sem.at[1, i]),
+            pltpu.make_async_copy(b_buf.at[at], b_out.at[at], out_sem.at[0, i]),
+            pltpu.make_async_copy(a_buf.at[at], a_out.at[at], out_sem.at[1, i]),
+        )
+
+    for i in range(PIECES):
+        copies(i)[0].start()
+        copies(i)[1].start()
+    for i in range(PIECES):
+        for k in range(2):
+            copies(i)[k].wait()
+            copies(i)[k + 2].start()
+    for i in range(PIECES):
+        copies(i)[2].wait()
+        copies(i)[3].wait()
 
 
 def fused(
@@ -900,7 +922,12 @@
         ),
         in_specs=[away, away],
         out_specs=(away, away),
-        scratch_shapes=[dma, dma],
+        scratch_shapes=[
+            pltpu.VMEM((rows, width), BF16),
+            pltpu.VMEM((rows, half), BF16),
+            dma((2, PIECES)),
+            dma((2, PIECES)),
+        ],
         compiler_params=pltpu.CompilerParams(vmem_limit_bytes=60 * 1024 * 1024),
     )(head_outputs, hidden)
     return (head_outputs[None], hidden)

time: 106 us -> 63.7 us (0.60)
  Pallas kernels: 105 us -> 62.9 us
    pallas_call x1, Pallas kernels: 44.8 us -> 2.26 us  [fused(): pl.pallas_call(handed_on, out_shape=(jax.ShapeDtypeStruct((rows, width),...]
where the time goes in v3:
time: 63.7 us; the launch traced here: 63.5 us
  Pallas kernels  62.9 us (99%)
  between operations  0.64 us (1%)
    pallas_call x1, Pallas kernels, fused(): pl.pallas_call(functools.partial(kernel, n), out_shape=(jax.ShapeDtypeStr...  60.6 us
    pallas_call x1, Pallas kernels, fused(): pl.pallas_call(handed_on, out_shape=(jax.ShapeDtypeStruct((rows, width),...  2.26 us

profile of v3, /device:TPU:25, one launch (start us, length us, event | category | flops | bytes accessed | tf_op | source)
XLA Modules:
  0.0 63.5 jit_solution(10169705636995214027)
XLA Ops:
  0.6 60.6 %shard_map.113 = (bf16[256,1024]{1,0:T(8,128)(2,1)}, bf16[256,1792]{1,0:T(8,128)(2,1)}) custom-call(bf16[256,1792]{1,0:T(8,128)(2,1)} %residual.1, bf16[256,1024]{1,0:T(8,128)(2,1)} %bitcast.7, bf16[256,256]{1,0:T(8,128)(2,1)} %bitcast.8, bf16[256,256]{1,0:T(8,128)(2,1)} %window_values.1, bf16[1024,3584]{1,0:T(8,128)(2,1)} %bitcast.6, bf16[3584]{0:T(1024)(128)(2,1)} %gain.1, ...), custom_call_target="tpu_custom_call" | custom-call | tf_op jit(solution)/shard_map/pallas_call | solution.py:834
  61.3 2.3 %shard_map.114 = (bf16[256,1024]{1,0:T(8,128)(2,1)}, bf16[256,1792]{1,0:T(8,128)(2,1)}) custom-call(bf16[256,1024]{1,0:T(8,128)(2,1)} %get-tuple-element.6.a, bf16[256,1792]{1,0:T(8,128)(2,1)} %get-tuple-element.7.b), custom_call_target="tpu_custom_call" | custom-call | tf_op jit(solution)/shard_map/pallas_call | solution.py:917

commit v4 on v3

--- a/solution.py
+++ b/solution.py
@@ -459,23 +459,23 @@
         allowed = key_index < lengths[c - slot]
         if first:
             allowed = allowed & (key_index <= lax.broadcasted_iota(jnp.int32, (rows, rows), 1))
-        for h in range(group):
-            at = slice(h * rows, (h + 1) * rows)
-            scores = jnp.where(allowed, nt(key_rows, stacked[at, :]), -1e30)
-            best = jnp.max(scores, axis=0, keepdims=True)
-            if not first:
-                best = jnp.maximum(best, top[:, at])
-            part = jnp.exp2((scores - best) * factor)
-            part_sum = jnp.sum(part, axis=0, keepdims=True)
-            blended = nn(value_t, part.astype(BF16))
+        spans = [slice(h * rows, (h + 1) * rows) for h in range(group)]
+        scores = [jnp.where(allowed, nt(key_rows, stacked[at, :]), -1e30) for at in spans]
+        best = [jnp.max(x, axis=0, keepdims=True) for x in scores]
+        if not first:
+            best = [jnp.maximum(x, top[:, at]) for x, at in zip(best, spans)]
+        parts = [jnp.exp2((x - b) * factor) for x, b in zip(scores, best)]
+        blended = [nn(value_t, x.astype(BF16)) for x in parts]
+        sums = [jnp.sum(x, axis=0, keepdims=True) for x in parts]
+        for h, at in enumerate(spans):
             if first:
-                total[:, at] = part_sum
-                blend[:, at] = blended
+                total[:, at] = sums[h]
+                blend[:, at] = blended[h]
             else:
-                shrink = jnp.exp2((top[:, at] - best) * factor)
-                total[:, at] = total[:, at] * shrink + part_sum
-                blend[:, at] = blend[:, at] * shrink + blended
-            top[:, at] = best
+                shrink = jnp.exp2((top[:, at] - best[h]) * factor)
+                total[:, at] = total[:, at] * shrink + sums[h]
+                blend[:, at] = blend[:, at] * shrink + blended[h]
+            top[:, at] = best[h]
 
     attend(0, True)
 
@@ -487,17 +487,23 @@
             along(k).start()
 
         across(k).start()
-        arrival(2 * k - 1).wait_recv()
-        attend(2 * k - 1, False)
         attend(2 * k, False)
+        behind = 2 * k - 3 + 2 * odd
+
+        @pl.when(behind > 0)
+        def _():
+            arrival(behind).wait_recv()
+            attend(behind, False)
+
         return carry
 
     lax.fori_loop(1, before + 1, attend_pair, 0)
-
-    @pl.when(odd == 1)
-    def _():
-        arrival(c).wait_recv()
-        attend(c, False)
+    rest_slot = 2 * before - 1 + 2 * odd
+
+    @pl.when(rest_slot > 0)
+    def _():
+        arrival(rest_slot).wait_recv()
+        attend(rest_slot, False)
 
     row_lane = lax.broadcasted_iota(jnp.int32, (1, rows), 1)
     for h in range(group):

time: 63.7 us -> 62.1 us (0.975)
  Pallas kernels: 62.9 us -> 61.3 us
    pallas_call x1, Pallas kernels: 60.6 us -> 59 us  [fused(): pl.pallas_call(functools.partial(kernel, n), out_shape=(jax.ShapeDtypeStr...]
where the time goes in v4:
time: 62.1 us; the launch traced here: 61.9 us
  Pallas kernels  61.3 us (99%)
  between operations  0.64 us (1%)
    pallas_call x1, Pallas kernels, fused(): pl.pallas_call(functools.partial(kernel, n), out_shape=(jax.ShapeDtypeStr...  59 us
    pallas_call x1, Pallas kernels, fused(): pl.pallas_call(handed_on, out_shape=(jax.ShapeDtypeStruct((rows, width),...  2.26 us

profile of v4, /device:TPU:25, one launch (start us, length us, event | category | flops | bytes accessed | tf_op | source)
XLA Modules:
  0.0 61.9 jit_solution(10739418832179441395)
XLA Ops:
  0.6 59.0 %shard_map.113 = (bf16[256,1024]{1,0:T(8,128)(2,1)}, bf16[256,1792]{1,0:T(8,128)(2,1)}) custom-call(bf16[256,1792]{1,0:T(8,128)(2,1)} %residual.1, bf16[256,1024]{1,0:T(8,128)(2,1)} %bitcast.7, bf16[256,256]{1,0:T(8,128)(2,1)} %bitcast.8, bf16[256,256]{1,0:T(8,128)(2,1)} %window_values.1, bf16[1024,3584]{1,0:T(8,128)(2,1)} %bitcast.6, bf16[3584]{0:T(1024)(128)(2,1)} %gain.1, ...), custom_call_target="tpu_custom_call" | custom-call | tf_op jit(solution)/shard_map/pallas_call | solution.py:840
  59.7 2.3 %shard_map.114 = (bf16[256,1024]{1,0:T(8,128)(2,1)}, bf16[256,1792]{1,0:T(8,128)(2,1)}) custom-call(bf16[256,1024]{1,0:T(8,128)(2,1)} %get-tuple-element.6.a, bf16[256,1792]{1,0:T(8,128)(2,1)} %get-tuple-element.7.b), custom_call_target="tpu_custom_call" | custom-call | tf_op jit(solution)/shard_map/pallas_call | solution.py:923

commit v5 on v4

--- a/solution.py
+++ b/solution.py
@@ -284,8 +284,8 @@
     states,
     fresh,
     incoming,
-    passed,
     mixed,
+    gate,
     gain_row,
     decay_wide,
     weights_sem,
@@ -329,9 +329,9 @@
         barrier, inc=1, device_id={"section": 1 - s, "tp": 1 - p}, device_id_type=MESH
     )
     pl.semaphore_signal(barrier, inc=1, device_id={"ctx": partner}, device_id_type=MESH)
-    for k in range(1, n // 2):
+    for shift in (2, n - 2):
         pl.semaphore_signal(
-            barrier, inc=1, device_id={"ctx": (c + 2 * k) % n}, device_id_type=MESH
+            barrier, inc=1, device_id={"ctx": lax.rem(c + shift, n)}, device_id_type=MESH
         )
 
     weights_copy = pltpu.make_async_copy(mixing, weights, weights_sem)
@@ -354,7 +354,7 @@
         kv[0, rows : rows + HEAD] = value_t[:, 0:HEAD]
         kv[0, rows + HEAD : rows + 2 * HEAD] = value_t[:, HEAD : 2 * HEAD]
 
-    pl.semaphore_wait(barrier, 3 + n // 2)
+    pl.semaphore_wait(barrier, 6)
 
     key_copy = pltpu.make_async_remote_copy(
         src_ref=keys.at[:, HEAD : 2 * HEAD],
@@ -603,7 +603,7 @@
         cum = jnp.transpose(cum_t)
         gain_row[...] = gain[...].astype(F32).reshape(1, 2 * half)
         last = cum[rows - 1 : rows, :]
-        rest[...] = jnp.exp(last - cum)
+        left = jnp.exp(last - cum)
         for g in range(2):
             masked = jnp.where(valid_col, keys[:, g * HEAD : (g + 1) * HEAD].astype(F32), 0.0)
             keys_t[g] = jnp.transpose(masked).astype(BF16)
@@ -613,6 +613,7 @@
             row = cum_t[h : h + 1, :]
             query = queries[:, at]
             damping = jnp.where(r >= t, jnp.exp(jnp.minimum(col - row, 0.0)), 0.0)
+            rest[:, at] = jnp.broadcast_to(left[:, h : h + 1], (rows, HEAD))
             damped[h] = (nn(query, keys_t[h // group]) * damping).astype(BF16)
             faded[:, at] = (query.astype(F32) * jnp.exp(col)).astype(BF16)
             sum_row = jnp.broadcast_to(last[:, h : h + 1], (PAD, HEAD))
@@ -624,6 +625,11 @@
                 high.astype(F32),
                 low,
             ).astype(BF16)
+        spike_copy.wait()
+        for h in range(heads):
+            at = slice(h * HEAD, (h + 1) * HEAD)
+            gated = spike_buf[:, at].astype(F32) * thresholds[:, at]
+            gate[:, at] = jnp.where(valid_col, gated, 0.0)
         values_sum[...] = jnp.zeros_like(values_sum)
         square_sum[...] = jnp.zeros_like(square_sum)
         weights_copy.wait()
@@ -667,13 +673,13 @@
                 device_id_type=MESH,
             )
 
-        def onward(k, g):
+        def onward(g):
             return pltpu.make_async_remote_copy(
-                src_ref=states.at[2, g],
-                dst_ref=states.at[2 + k, g],
-                send_sem=state_send.at[k, g],
-                recv_sem=state_recv.at[k, g],
-                device_id={"ctx": lax.rem(c + 2 * k, n)},
+                src_ref=states.at[2, g, 0:HEAD],
+                dst_ref=states.at[3, g, 0:HEAD],
+                send_sem=state_send.at[g],
+                recv_sem=state_recv.at[g],
+                device_id={"ctx": lax.rem(c + 2, n)},
                 device_id_type=MESH,
             )
 
@@ -687,7 +693,7 @@
         for g in range(2):
             for h in range(g * group, (g + 1) * group):
                 at = slice(h * HEAD, (h + 1) * HEAD)
-                weighted = (values[:, at].astype(F32) * rest[:, h : h + 1]).astype(BF16)
+                weighted = (values[:, at].astype(F32) * rest[:, at]).astype(BF16)
                 fresh[:, at] = nn(keys_t[g], weighted)
                 in_group = slice((h % group) * HEAD, (h % group + 1) * HEAD)
                 states[0, g, 0:HEAD, in_group] = fresh[:, at].astype(BF16)
@@ -709,55 +715,39 @@
 
             @pl.when(here_later > 0)
             def _():
-                own_sum = sum_of(0, g)
-                other_sum = sum_of(1, g)
-                second = jnp.where(odd == 1, own_sum, other_sum)
                 own = fresh[:, at]
                 other = states[1, g, 0:HEAD, :].astype(F32)
+                second = jnp.where(odd == 1, sum_of(0, g), sum_of(1, g))
                 first_part = jnp.where(odd == 1, other, own)
                 second_part = jnp.where(odd == 1, own, other)
-                states[2, g, 0:HEAD, :] = (first_part * jnp.exp(second) + second_part).astype(BF16)
-                both_sum = jnp.broadcast_to(own_sum + other_sum, (PAD, wide))
-                high = both_sum.astype(BF16).astype(F32)
-                states[2, g, HEAD : HEAD + PAD, :] = jnp.where(
-                    lax.broadcasted_iota(jnp.int32, (PAD, wide), 0) < PAD // 2,
-                    high,
-                    both_sum - high,
-                ).astype(BF16)
-
-                def send_on(k, carry):
-                    onward(k, g).start()
-                    return carry
-
-                lax.fori_loop(1, here_later + 1, send_on, 0)
-
-        spike_copy.wait()
-        for g in range(2):
-            at = slice(g * wide, (g + 1) * wide)
+                fresh[:, at] = first_part * jnp.exp(second) + second_part
+
+            @pl.when(before > 0)
+            def _():
+                onward(g).wait_recv()
+                incoming[:, at] = states[3, g, 0:HEAD, :].astype(F32)
+
+            @pl.when(before == 0)
+            def _():
+                incoming[:, at] = jnp.zeros((HEAD, wide), F32)
+
+            @pl.when(here_later > 0)
+            def _():
+                faded_in = incoming[:, at] * jnp.exp(sum_of(0, g) + sum_of(1, g))
+                states[2, g, 0:HEAD, :] = (faded_in + fresh[:, at]).astype(BF16)
+                onward(g).start()
 
             @pl.when(odd == 1)
             def _():
-                incoming[:, at] = states[1, g, 0:HEAD, :].astype(F32)
-                passed[:, at] = sum_of(1, g)
-
-            @pl.when(odd == 0)
-            def _():
-                incoming[:, at] = jnp.zeros((HEAD, wide), F32)
-                passed[:, at] = jnp.zeros((1, wide), F32)
-
-            def join(k, carry):
-                onward(k, g).wait_recv()
-                incoming[:, at] += states[2 + k, g, 0:HEAD, :].astype(F32) * jnp.exp(passed[:, at])
-                passed[:, at] += sum_of(2 + k, g)
-                return carry
-
-            lax.fori_loop(1, before + 1, join, 0)
+                incoming[:, at] = incoming[:, at] * jnp.exp(sum_of(1, g)) + states[
+                    1, g, 0:HEAD, :
+                ].astype(F32)
+
             for h in range(g * group, (g + 1) * group):
                 at = slice(h * HEAD, (h + 1) * HEAD)
                 both = mixed[:, at] + nn(faded[:, at], incoming[:, at].astype(BF16))
                 scaled = both * lax.rsqrt(jnp.mean(both * both, axis=1, keepdims=True) + 1e-05)
-                gated = scaled * (spike_buf[:, at].astype(F32) * thresholds[:, at])
-                head_out[:, at] = jnp.where(valid_col, gated, 0.0).astype(BF16)
+                head_out[:, at] = (scaled * gate[:, at]).astype(BF16)
 
         for g in range(2):
 
@@ -765,11 +755,10 @@
             def _():
                 swap(g).wait_send()
 
-            def sent_on(k, carry):
-                onward(k, g).wait_send()
-                return carry
-
-            lax.fori_loop(1, here_later + 1, sent_on, 0)
+            @pl.when(here_later > 0)
+            def _():
+                onward(g).wait_send()
+
         each(chunks_half, lambda j: hid(j).wait_send())
         residual_send.wait_send()
         att_copy.wait_send()
@@ -875,13 +864,13 @@
             pltpu.VMEM((rows, 1), F32),
             pltpu.VMEM((heads, rows, rows), BF16),
             pltpu.VMEM((rows, width), BF16),
-            pltpu.VMEM((rows, HEAD), F32),
+            pltpu.VMEM((rows, width), F32),
             pltpu.VMEM((2, HEAD, rows), BF16),
             pltpu.VMEM((rows, width), BF16),
-            pltpu.VMEM((n // 2 + 2, 2, HEAD + PAD, width // 2), BF16),
+            pltpu.VMEM((4, 2, HEAD + PAD, width // 2), BF16),
             pltpu.VMEM((HEAD, width), F32),
             pltpu.VMEM((HEAD, width), F32),
-            pltpu.VMEM((1, width), F32),
+            pltpu.VMEM((rows, width), F32),
             pltpu.VMEM((rows, width), F32),
             pltpu.VMEM((1, 2 * half), F32),
             pltpu.VMEM((HEAD, rows), F32),
@@ -902,8 +891,8 @@
             dma((chunks // 2,)),
             dma((2,)),
             dma((2,)),
-            dma((n // 2, 2)),
-            dma((n // 2, 2)),
+            dma((2,)),
+            dma((2,)),
         ],
         compiler_params=pltpu.CompilerParams(
             collective_id=0, has_side_effects=True, vmem_limit_bytes=56 * 1024 * 1024
@@ -951,6 +940,7 @@
         and rows == 2 * HEAD
         and residual.shape[1] % CHUNK == 0
         and shards % 2 == 0
+        and shards >= 4
         and shards * rows <= WINDOW
     )
     return fused(*arrays) if fits else body(*arrays)

time: 62.1 us -> 56.5 us (0.910)
  Pallas kernels: 61.3 us -> 55.2 us
    pallas_call x1, Pallas kernels: 59 us -> 52.9 us  [fused(): pl.pallas_call(functools.partial(kernel, n), out_shape=(jax.ShapeDtypeStr...]
where the time goes in v5:
time: 56.5 us; the launch traced here: 55.8 us
  Pallas kernels  55.2 us (98%)
  between operations  0.64 us (1%)
    pallas_call x1, Pallas kernels, fused(): pl.pallas_call(functools.partial(kernel, n), out_shape=(jax.ShapeDtypeStr...  52.9 us
    pallas_call x1, Pallas kernels, fused(): pl.pallas_call(handed_on, out_shape=(jax.ShapeDtypeStruct((rows, width),...  2.26 us

profile of v5, /device:TPU:25, one launch (start us, length us, event | category | flops | bytes accessed | tf_op | source)
XLA Modules:
  0.0 55.8 jit_solution(4546242147198506855)
XLA Ops:
  0.6 52.9 %shard_map.113 = (bf16[256,1024]{1,0:T(8,128)(2,1)}, bf16[256,1792]{1,0:T(8,128)(2,1)}) custom-call(bf16[256,1792]{1,0:T(8,128)(2,1)} %residual.1, bf16[256,1024]{1,0:T(8,128)(2,1)} %bitcast.7, bf16[256,256]{1,0:T(8,128)(2,1)} %bitcast.8, bf16[256,256]{1,0:T(8,128)(2,1)} %window_values.1, bf16[1024,3584]{1,0:T(8,128)(2,1)} %bitcast.6, bf16[3584]{0:T(1024)(128)(2,1)} %gain.1, ...), custom_call_target="tpu_custom_call" | custom-call | tf_op jit(solution)/shard_map/pallas_call | solution.py:829
  53.6 2.3 %shard_map.114 = (bf16[256,1024]{1,0:T(8,128)(2,1)}, bf16[256,1792]{1,0:T(8,128)(2,1)}) custom-call(bf16[256,1024]{1,0:T(8,128)(2,1)} %get-tuple-element.6.a, bf16[256,1792]{1,0:T(8,128)(2,1)} %get-tuple-element.7.b), custom_call_target="tpu_custom_call" | custom-call | tf_op jit(solution)/shard_map/pallas_call | solution.py:912

commit v6 on v5

--- a/solution.py
+++ b/solution.py
@@ -230,7 +230,7 @@
 F32 = jnp.float32
 BF16 = jnp.bfloat16
 CHUNK = 256
-PAD = 16
+PAD = 8
 PIECES = 4
 
 
@@ -286,6 +286,7 @@
     incoming,
     mixed,
     gate,
+    totals,
     gain_row,
     decay_wide,
     weights_sem,
@@ -303,6 +304,7 @@
     term_far_recv,
     hid_send,
     hid_recv,
+    totals_sem,
     swap_send,
     swap_recv,
     state_send,
@@ -391,10 +393,57 @@
     residual_copy = pltpu.make_async_copy(residual, residuals.at[p], res_sem.at[2])
     spike_copy = pltpu.make_async_copy(spikes, spike_buf, spike_sem)
 
+    def along(k, part):
+        at = slice(part * rows, (part + 1) * rows)
+        return pltpu.make_async_remote_copy(
+            src_ref=kv.at[2 * k, at],
+            dst_ref=kv.at[2 * k + 2, at],
+            send_sem=kv_send.at[k, part],
+            recv_sem=kv_recv.at[2 * k + 2, part],
+            device_id={"ctx": lax.rem(c + 2, n)},
+            device_id_type=MESH,
+        )
+
+    def across(k, part):
+        at = slice(part * rows, (part + 1) * rows)
+        return pltpu.make_async_remote_copy(
+            src_ref=kv.at[2 * k, at],
+            dst_ref=kv.at[2 * k + step_to, at],
+            send_sem=kv_forward.at[k, part],
+            recv_sem=kv_recv.at[2 * k + step_to, part],
+            device_id={"ctx": partner},
+            device_id_type=MESH,
+        )
+
+    def arrival(slot, part):
+        at = slice(part * rows, (part + 1) * rows)
+        return pltpu.make_async_remote_copy(
+            src_ref=kv.at[slot, at],
+            dst_ref=kv.at[slot, at],
+            send_sem=kv_send.at[0, part],
+            recv_sem=kv_recv.at[slot, part],
+            device_id={"ctx": partner},
+            device_id_type=MESH,
+        )
+
+    before = c // 2
+    pairs = n // 2
+
+    def send_own(part):
+        @pl.when(c + 2 < n)
+        def _():
+            along(0, part).start()
+
+        @pl.when(odd == 0)
+        def _():
+            across(0, part).start()
+
     @pl.when(s == 0)
     def _():
         key_copy.start()
         query_copy.start()
+
+    send_own(1)
 
     @pl.when(s == 1)
     def _():
@@ -403,46 +452,7 @@
         spike_copy.start()
         key_copy.wait_recv()
 
-    def along(k):
-        return pltpu.make_async_remote_copy(
-            src_ref=kv.at[2 * k],
-            dst_ref=kv.at[2 * k + 2],
-            send_sem=kv_send.at[k],
-            recv_sem=kv_recv.at[2 * k + 2],
-            device_id={"ctx": lax.rem(c + 2, n)},
-            device_id_type=MESH,
-        )
-
-    def across(k):
-        return pltpu.make_async_remote_copy(
-            src_ref=kv.at[2 * k],
-            dst_ref=kv.at[2 * k + step_to],
-            send_sem=kv_forward.at[k],
-            recv_sem=kv_recv.at[2 * k + step_to],
-            device_id={"ctx": partner},
-            device_id_type=MESH,
-        )
-
-    def arrival(slot):
-        return pltpu.make_async_remote_copy(
-            src_ref=kv.at[slot],
-            dst_ref=kv.at[slot],
-            send_sem=kv_send.at[0],
-            recv_sem=kv_recv.at[slot],
-            device_id={"ctx": partner},
-            device_id_type=MESH,
-        )
-
-    before = c // 2
-    pairs = n // 2
-
-    @pl.when(c + 2 < n)
-    def _():
-        along(0).start()
-
-    @pl.when(odd == 0)
-    def _():
-        across(0).start()
+    send_own(0)
 
     @pl.when(s == 1)
     def _():
@@ -480,19 +490,21 @@
     attend(0, True)
 
     def attend_pair(k, carry):
-        arrival(2 * k).wait_recv()
-
-        @pl.when(c + 2 < n)
-        def _():
-            along(k).start()
-
-        across(k).start()
+        for part in (1, 0):
+            arrival(2 * k, part).wait_recv()
+
+            @pl.when(c + 2 < n)
+            def _():
+                along(k, part).start()
+
+            across(k, part).start()
         attend(2 * k, False)
         behind = 2 * k - 3 + 2 * odd
 
         @pl.when(behind > 0)
         def _():
-            arrival(behind).wait_recv()
+            arrival(behind, 1).wait_recv()
+            arrival(behind, 0).wait_recv()
             attend(behind, False)
 
         return carry
@@ -502,7 +514,8 @@
 
     @pl.when(rest_slot > 0)
     def _():
-        arrival(rest_slot).wait_recv()
+        arrival(rest_slot, 1).wait_recv()
+        arrival(rest_slot, 0).wait_recv()
         attend(rest_slot, False)
 
     row_lane = lax.broadcasted_iota(jnp.int32, (1, rows), 1)
@@ -567,13 +580,13 @@
             at = pl.ds(pl.multiple_of(j * CHUNK, CHUNK), CHUNK)
             both = jnp.concatenate([attention[0], attention[1]], axis=1)
             terms[j] = nn(both, weights[:, at]).astype(BF16)
+
+            @pl.when(j >= 2)
+            def _():
+                term_far(j - 2).wait_send()
+
+            term_far(j).start()
             term_own(j).start()
-
-            @pl.when(j >= 2)
-            def _():
-                term_far(j - 2).wait_send()
-
-            term_far(j).start()
             return carry
 
         lax.fori_loop(0, chunks, project, 0)
@@ -616,15 +629,16 @@
             rest[:, at] = jnp.broadcast_to(left[:, h : h + 1], (rows, HEAD))
             damped[h] = (nn(query, keys_t[h // group]) * damping).astype(BF16)
             faded[:, at] = (query.astype(F32) * jnp.exp(col)).astype(BF16)
-            sum_row = jnp.broadcast_to(last[:, h : h + 1], (PAD, HEAD))
-            high = sum_row.astype(BF16)
-            low = sum_row - high.astype(F32)
-            in_group = slice((h % group) * HEAD, (h % group + 1) * HEAD)
-            states[0, h // group, HEAD : HEAD + PAD, in_group] = jnp.where(
-                lax.broadcasted_iota(jnp.int32, (PAD, HEAD), 0) < PAD // 2,
-                high.astype(F32),
-                low,
-            ).astype(BF16)
+            totals[0, :, at] = jnp.broadcast_to(last[:, h : h + 1], (PAD, HEAD))
+        totals_copy = pltpu.make_async_remote_copy(
+            src_ref=totals.at[0],
+            dst_ref=totals.at[1],
+            send_sem=totals_sem.at[0],
+            recv_sem=totals_sem.at[1],
+            device_id={"ctx": partner},
+            device_id_type=MESH,
+        )
+        totals_copy.start()
         spike_copy.wait()
         for h in range(heads):
             at = slice(h * HEAD, (h + 1) * HEAD)
@@ -675,8 +689,8 @@
 
         def onward(g):
             return pltpu.make_async_remote_copy(
-                src_ref=states.at[2, g, 0:HEAD],
-                dst_ref=states.at[3, g, 0:HEAD],
+                src_ref=states.at[2, g],
+                dst_ref=states.at[3, g],
                 send_sem=state_send.at[g],
                 recv_sem=state_recv.at[g],
                 device_id={"ctx": lax.rem(c + 2, n)},
@@ -684,8 +698,7 @@
             )
 
         def sum_of(slot, g):
-            rows_of = states[slot, g, HEAD : HEAD + PAD, :].astype(F32)
-            return rows_of[0:1, :] + rows_of[PAD // 2 : PAD // 2 + 1, :]
+            return totals[slot, 0:1, g * wide : (g + 1) * wide]
 
         here_later = pairs - 1 - before
         swap_out = (odd == 0) | (here_later > 0)
@@ -706,6 +719,8 @@
             at = slice(h * HEAD, (h + 1) * HEAD)
             mixed[:, at] = nn(damped[h], values[:, at])
 
+        totals_copy.wait_recv()
+
         for g in range(2):
             at = slice(g * wide, (g + 1) * wide)
 
@@ -761,10 +776,12 @@
 
         each(chunks_half, lambda j: hid(j).wait_send())
         residual_send.wait_send()
+        totals_copy.wait_send()
         att_copy.wait_send()
 
     def along_done(k, carry):
-        along(k).wait_send()
+        along(k, 0).wait_send()
+        along(k, 1).wait_send()
         return carry
 
     @pl.when(c + 2 < n)
@@ -773,10 +790,12 @@
 
     @pl.when(odd == 0)
     def _():
-        across(0).wait_send()
+        across(0, 0).wait_send()
+        across(0, 1).wait_send()
 
     def across_done(k, carry):
-        across(k).wait_send()
+        across(k, 0).wait_send()
+        across(k, 1).wait_send()
         return carry
 
     lax.fori_loop(1, before + 1, across_done, 0)
@@ -867,11 +886,12 @@
             pltpu.VMEM((rows, width), F32),
             pltpu.VMEM((2, HEAD, rows), BF16),
             pltpu.VMEM((rows, width), BF16),
-            pltpu.VMEM((4, 2, HEAD + PAD, width // 2), BF16),
+            pltpu.VMEM((4, 2, HEAD, width // 2), BF16),
             pltpu.VMEM((HEAD, width), F32),
             pltpu.VMEM((HEAD, width), F32),
             pltpu.VMEM((rows, width), F32),
             pltpu.VMEM((rows, width), F32),
+            pltpu.VMEM((2, PAD, width), F32),
             pltpu.VMEM((1, 2 * half), F32),
             pltpu.VMEM((HEAD, rows), F32),
             dma,
@@ -879,9 +899,9 @@
             dma((3,)),
             dma((2,)),
             dma((2,)),
-            dma((n // 2,)),
-            dma((n,)),
-            dma((n // 2,)),
+            dma((n // 2, 2)),
+            dma((n, 2)),
+            dma((n // 2, 2)),
             dma((2,)),
             dma((chunks,)),
             dma((chunks,)),
@@ -889,6 +909,7 @@
             dma((chunks,)),
             dma((chunks // 2,)),
             dma((chunks // 2,)),
+            dma((2,)),
             dma((2,)),
             dma((2,)),
             dma((2,)),

time: 56.5 us -> 55.7 us (0.986)
  no operation moved by 1% of the time
where the time goes in v6:
time: 55.7 us; the launch traced here: 55.6 us
  Pallas kernels  54.9 us (99%)
  between operations  0.64 us (1%)
    pallas_call x1, Pallas kernels, fused(): pl.pallas_call(functools.partial(kernel, n), out_shape=(jax.ShapeDtypeStr...  52.7 us
    pallas_call x1, Pallas kernels, fused(): pl.pallas_call(handed_on, out_shape=(jax.ShapeDtypeStruct((rows, width),...  2.26 us

profile of v6, /device:TPU:25, one launch (start us, length us, event | category | flops | bytes accessed | tf_op | source)
XLA Modules:
  0.0 55.6 jit_solution(7865351801466254559)
XLA Ops:
  0.6 52.7 %shard_map.113 = (bf16[256,1024]{1,0:T(8,128)(2,1)}, bf16[256,1792]{1,0:T(8,128)(2,1)}) custom-call(bf16[256,1792]{1,0:T(8,128)(2,1)} %residual.1, bf16[256,1024]{1,0:T(8,128)(2,1)} %bitcast.7, bf16[256,256]{1,0:T(8,128)(2,1)} %bitcast.8, bf16[256,256]{1,0:T(8,128)(2,1)} %window_values.1, bf16[1024,3584]{1,0:T(8,128)(2,1)} %bitcast.6, bf16[3584]{0:T(1024)(128)(2,1)} %gain.1, ...), custom_call_target="tpu_custom_call" | custom-call | tf_op jit(solution)/shard_map/pallas_call | solution.py:848
  53.3 2.3 %shard_map.114 = (bf16[256,1024]{1,0:T(8,128)(2,1)}, bf16[256,1792]{1,0:T(8,128)(2,1)}) custom-call(bf16[256,1024]{1,0:T(8,128)(2,1)} %get-tuple-element.6.a, bf16[256,1792]{1,0:T(8,128)(2,1)} %get-tuple-element.7.b), custom_call_target="tpu_custom_call" | custom-call | tf_op jit(solution)/shard_map/pallas_call | solution.py:933

commit v7 on v6

--- a/solution.py
+++ b/solution.py
@@ -274,6 +274,7 @@
     far_terms,
     residuals,
     hidden_buf,
+    current,
     values_sum,
     square_sum,
     damped,
@@ -426,6 +427,8 @@
             device_id_type=MESH,
         )
 
+    late_one = c // (n // 2)
+    late = late_one == 1
     before = c // 2
     pairs = n // 2
 
@@ -447,7 +450,11 @@
 
     @pl.when(s == 1)
     def _():
-        residual_send.start()
+
+        @pl.when(late)
+        def _():
+            residual_send.start()
+
         residual_copy.start()
         spike_copy.start()
         key_copy.wait_recv()
@@ -564,6 +571,16 @@
             device_id_type=MESH,
         )
 
+    def hid_across(j):
+        return pltpu.make_async_remote_copy(
+            src_ref=hidden_buf.at[j],
+            dst_ref=far_terms.at[p * chunks_half + j],
+            send_sem=term_far_send.at[p * chunks_half + j],
+            recv_sem=term_far_recv.at[p * chunks_half + j],
+            device_id={"tp": 1 - p},
+            device_id_type=MESH,
+        )
+
     def each(count, act):
         def one(j, carry):
             act(j)
@@ -576,25 +593,39 @@
         weights_copy.wait()
         att_copy.wait_recv()
 
-        def project(j, carry):
+        def project(i, carry):
+            flip = 1 - i % 2
+            side = p + flip - 2 * p * flip
+            j = side * chunks_half + i // 2
             at = pl.ds(pl.multiple_of(j * CHUNK, CHUNK), CHUNK)
             both = jnp.concatenate([attention[0], attention[1]], axis=1)
             terms[j] = nn(both, weights[:, at]).astype(BF16)
 
-            @pl.when(j >= 2)
-            def _():
-                term_far(j - 2).wait_send()
-
-            term_far(j).start()
-            term_own(j).start()
+            @pl.when((flip == 1) | late)
+            def _():
+                term_far(j).start()
+
+            @pl.when((flip == 0) | late)
+            def _():
+                term_own(j).start()
+
+            return carry
+
+        def sent(j, carry):
+            @pl.when((j // chunks_half != p) | late)
+            def _():
+                term_far(j).wait_send()
+
+            @pl.when((j // chunks_half == p) | late)
+            def _():
+                term_own(j).wait_send()
+
             return carry
 
         lax.fori_loop(0, chunks, project, 0)
         head_out[:, 0:wide] = attention[0]
         head_out[:, wide : 2 * wide] = attention[1]
-        term_far(chunks - 2).wait_send()
-        term_far(chunks - 1).wait_send()
-        each(chunks, lambda j: term_own(j).wait_send())
+        lax.fori_loop(0, chunks, sent, 0)
         key_copy.wait_send()
         query_copy.wait_send()
         each(chunks_half, lambda j: hid(j).wait_recv())
@@ -648,24 +679,43 @@
         square_sum[...] = jnp.zeros_like(square_sum)
         weights_copy.wait()
         residual_copy.wait()
-        residual_recv.wait_recv()
-
-        def collect(j, carry):
-            side = j // chunks_half
-            col = j - side * chunks_half
+
+        @pl.when(late)
+        def _():
+            residual_recv.wait_recv()
+
+        def collect(i, carry):
+            col = late_one * (i // 2) + (1 - late_one) * (i % chunks_half)
+            flip = late_one * (i % 2) + (1 - late_one) * (i // chunks_half)
+            side = p + flip - 2 * p * flip
+            j = side * chunks_half + col
             here = pl.ds(pl.multiple_of(col * CHUNK, CHUNK), CHUNK)
             at = pl.ds(pl.multiple_of(j * CHUNK, CHUNK), CHUNK)
-            term_own(j).wait_recv()
             term_far(j).wait_recv()
-            summed = residuals[side, :, here].astype(F32) + (
-                own_terms[j].astype(F32) + far_terms[j].astype(F32)
-            )
-            narrow = summed.astype(BF16)
-
-            @pl.when(side == p)
+
+            @pl.when((flip == 0) | late)
+            def _():
+                term_own(j).wait_recv()
+                summed = residuals[side, :, here].astype(F32) + (
+                    own_terms[j].astype(F32) + far_terms[j].astype(F32)
+                )
+                current[...] = summed.astype(BF16)
+
+            @pl.when((flip == 1) & (late_one == 0))
+            def _():
+                current[...] = far_terms[j]
+
+            narrow = current[...]
+
+            @pl.when(flip == 0)
             def _():
                 hidden_buf[col] = narrow
                 hidden_out[:, here] = narrow
+
+                @pl.when(late_one == 0)
+                def _():
+                    hid_across(col).start()
+
                 hid(col).start()
 
             rounded = narrow.astype(F32)
@@ -775,7 +825,15 @@
                 onward(g).wait_send()
 
         each(chunks_half, lambda j: hid(j).wait_send())
-        residual_send.wait_send()
+
+        @pl.when(late)
+        def _():
+            residual_send.wait_send()
+
+        @pl.when(late_one == 0)
+        def _():
+            each(chunks_half, lambda j: hid_across(j).wait_send())
+
         totals_copy.wait_send()
         att_copy.wait_send()
 
@@ -879,6 +937,7 @@
             pltpu.VMEM((chunks, rows, CHUNK), BF16),
             pltpu.VMEM((2, rows, half), BF16),
             pltpu.VMEM((chunks // 2, rows, CHUNK), BF16),
+            pltpu.VMEM((rows, CHUNK), BF16),
             pltpu.VMEM((rows, width), F32),
             pltpu.VMEM((rows, 1), F32),
             pltpu.VMEM((heads, rows, rows), BF16),

time: 55.7 us -> 53.4 us (0.959)
  Pallas kernels: 54.9 us -> 52.5 us
    pallas_call x1, Pallas kernels: 52.7 us -> 50.3 us  [fused(): pl.pallas_call(functools.partial(kernel, n), out_shape=(jax.ShapeDtypeStr...]
where the time goes in v7:
time: 53.4 us; the launch traced here: 53.2 us
  Pallas kernels  52.5 us (98%)
  between operations  0.64 us (1%)
    pallas_call x1, Pallas kernels, fused(): pl.pallas_call(functools.partial(kernel, n), out_shape=(jax.ShapeDtypeStr...  50.3 us
    pallas_call x1, Pallas kernels, fused(): pl.pallas_call(handed_on, out_shape=(jax.ShapeDtypeStruct((rows, width),...  2.26 us

profile of v7, /device:TPU:25, one launch (start us, length us, event | category | flops | bytes accessed | tf_op | source)
XLA Modules:
  0.0 53.2 jit_solution(2317296940819988347)
XLA Ops:
  0.6 50.3 %shard_map.113 = (bf16[256,1024]{1,0:T(8,128)(2,1)}, bf16[256,1792]{1,0:T(8,128)(2,1)}) custom-call(bf16[256,1792]{1,0:T(8,128)(2,1)} %residual.1, bf16[256,1024]{1,0:T(8,128)(2,1)} %bitcast.7, bf16[256,256]{1,0:T(8,128)(2,1)} %bitcast.8, bf16[256,256]{1,0:T(8,128)(2,1)} %window_values.1, bf16[1024,3584]{1,0:T(8,128)(2,1)} %bitcast.6, bf16[3584]{0:T(1024)(128)(2,1)} %gain.1, ...), custom_call_target="tpu_custom_call" | custom-call | tf_op jit(solution)/shard_map/pallas_call | solution.py:906
  50.9 2.3 %shard_map.114 = (bf16[256,1024]{1,0:T(8,128)(2,1)}, bf16[256,1792]{1,0:T(8,128)(2,1)}) custom-call(bf16[256,1024]{1,0:T(8,128)(2,1)} %get-tuple-element.6.a, bf16[256,1792]{1,0:T(8,128)(2,1)} %get-tuple-element.7.b), custom_call_target="tpu_custom_call" | custom-call | tf_op jit(solution)/shard_map/pallas_call | solution.py:992
